TPU v7x, 32 devices: a whole 2x2x4 slice. The times are simulated.
32 devices in a mesh: replica: 4 (over x, core), shard: 8 (over z, y).
Axes of the slice: x: 2, y: 2, z: 4, core: 2. Of those that a mesh axis runs over, the one named last changes fastest.
Arguments:
- tokens: bfloat16 [8192, 1088], P(('replica', 'shard')), may hold values from -6 to 6
- slot: int32 [8192], P(('replica', 'shard')), may hold values from 0 to 2047, as said below
- lengths: int32 [4, 6], P('replica'), may hold values from 1 to 1024, 2048 in all within a row
- attn_in_weight: bfloat16 [1088, 3264], P('shard'), may hold values from -0.1875 to 0.1875
- attn_out_weight: bfloat16 [1088, 1088], P('shard'), may hold values from -2.5 to 2.5
- up_weight: bfloat16 [1088, 4352], P('shard'), may hold values from -0.1875 to 0.1875
- down_weight: bfloat16 [4352, 1088], P('shard'), may hold values from -0.09375 to 0.09375
- norm_gains: float32 [2, 1088], replicated, may hold values from 0.1 to 1.9
- layer_biases: float32 [6, 1088], replicated, may hold values from -0.6 to 0.6
- up_bias: float32 [4352], replicated, may hold values from -3 to 3
- cotangent: bfloat16 [8192, 1088], P(('replica', 'shard')), may hold values from -6 to 6
Outputs:
- mixed: bfloat16 [8192, 1088], P(('replica', 'shard'))
- tokens_grad: float32 [8192, 1088], P(('replica', 'shard'))
- attn_in_grad: float32 [1088, 3264], P('shard')
- attn_out_grad: float32 [1088, 1088], P('shard')
- up_grad: float32 [1088, 4352], P('shard')
- down_grad: float32 [4352, 1088], P('shard')
- gains_grad: float32 [2, 1088], P(None, 'shard')
- biases_grad: float32 [6, 1088], P(None, 'shard')
- up_bias_grad: float32 [4352], P('shard')
Inputs may be any that keep to these rules, and one draw needn't show every extreme that they name: `slot`: within each group's rows (blocks of 2048 rows in order), every place 0 to 2047 occurs exactly once. Each row of lengths sums to 2048; its largest entry is 1024.
All inputs are finite; a program needn't handle non-finite values.
Results may differ from a plain program's by a relative error of at most 0.02.
Values may be sent and summed in bfloat16 or wider, within the bound.
No kernel may reach another device: no remote copies, remote signals or barrier semaphores. Data moves between devices by JAX's collectives and lax.ppermute only.
A program may use at most 256 MiB of HBM per device.

v0:
```python
import functools
import math

import jax
import jax.numpy as jnp
from jax import lax
from jax.experimental import pallas as pl
from jax.experimental.pallas import tpu as pltpu
from jax.sharding import Mesh, PartitionSpec as P

HEAD = 64
BF = jnp.bfloat16
F32 = jnp.float32
REP = ("x", "core")
SHARD = ("z", "y")
NEG = -1e30


def dot(left, right):
    return jnp.dot(left, right, preferred_element_type=F32)


def dot_nt(left, right):
    return lax.dot_general(left, right, (((1,), (1,)), ((), ())), preferred_element_type=F32)


def dot_tn(left, right):
    return lax.dot_general(left, right, (((0,), (0,)), ((), ())), preferred_element_type=F32)


def iota(shape, dim):
    return lax.broadcasted_iota(jnp.int32, shape, dim)


def doc_starts(places, ends_ref):
    starts = jnp.zeros_like(places)
    for n in range(ends_ref.shape[0]):
        starts = jnp.where(places >= ends_ref[n], ends_ref[n], starts)
    return starts


def first_block(block, tile, ends_ref):
    row = block * tile
    start = jnp.int32(0)
    for n in range(ends_ref.shape[0]):
        start = jnp.where(row >= ends_ref[n], ends_ref[n], start)
    return lax.div(start, jnp.int32(tile))


def rows(block, tile):
    return pl.ds(pl.multiple_of(block * tile, tile), tile)


def only_head(values, head):
    lanes = iota(values.shape, 1)
    keep = (lanes < HEAD) if head == 0 else (lanes >= HEAD)
    return jnp.where(keep, values, jnp.zeros_like(values))


def tail_slots(tail):
    lanes = iota(tail.shape, 1)
    spare = tail.shape[1] // 2
    weight = jnp.where(lanes == spare, 64.0, jnp.where(lanes == spare + 1, 1.0, 0.0))
    return tail.astype(F32) * weight


def forward_kernel(blocks, ends_ref, spot_ref, *refs):
    h_refs, refs = refs[:blocks], refs[blocks:]
    (
        wa_ref, wb_ref, bias_ref, own_ref,
        sp_ref, kt_ref, o_ref, of_ref, lse_ref, q16_ref, o16_ref, lse16_ref, w_ref, srow_ref, scol_ref,
        p_scr, vt_scr, ob_scr, row_scr,
    ) = refs
    tile = own_ref.shape[1]
    total = blocks * tile
    feats = wa_ref.shape[1]
    wide = in_width(feats, blocks)
    z, y, corner = spot_ref[0], spot_ref[1], spot_ref[2]
    zs = blocks // 2

    w_ref[...] = jnp.zeros_like(w_ref)
    for c in range(4):
        @pl.when(corner == c)
        def _(c=c):
            for n, (ref, at) in enumerate(((wa_ref, 0), (wa_ref, 1), (wb_ref, 0), (wb_ref, 1))):
                place = c ^ n
                w_ref[:feats, place * wide:(place + 1) * wide] = ref[at, :, :wide]

    me = z * 2 + y
    lanes = pl.ds(pl.multiple_of(me * 128, 128), 128)
    blank = jnp.zeros((1, 128), F32)
    last = bias_ref.shape[1] - HEAD
    bias = jnp.concatenate(
        [
            bias_ref[1:2, lanes], blank, bias_ref[2:3, lanes],
            blank[:, :HEAD], bias_ref[2:3, last:], bias_ref[1:2, last:], blank[:, :HEAD],
        ],
        axis=1,
    )
    for b in range(blocks):
        r = slice(b * tile, (b + 1) * tile)
        p_scr[r, :] = (dot(h_refs[b][...], w_ref[...]) + bias).astype(BF)
        tail = tail_slots(h_refs[b][:, h_refs[b].shape[1] - 128:])
        scol_ref[r, :] = jnp.sum(tail, axis=1, keepdims=True).astype(jnp.int32)
        row = jnp.sum(tail.T, axis=0, keepdims=True).astype(jnp.int32)
        row_scr[:, r] = row
        shard = lax.rem(z + zs - b // 2, zs) * 2 + lax.rem(y + b % 2, 2)
        srow_ref[shard] = row

    @pl.loop(0, blocks)
    def _(b):
        r = rows(b, tile)
        place = iota((tile, total), 0) + b * tile
        pick = jnp.where(row_scr[...] == place, 1.0, 0.0).astype(BF)
        sorted_f = dot(pick, p_scr[:, :512])
        sp_ref[r, :] = sorted_f.astype(BF)
        kt_ref[b] = sorted_f[:, 128:256].T.astype(BF)
        vt_scr[b, :128, :] = sorted_f[:, 256:384].T.astype(BF)
        vt_scr[b, 128:, :] = sorted_f[:, 384:512].T.astype(BF)

    q16 = p_scr[0:tile, 512:640]
    q16_ref[...] = q16

    own = own_ref[...]
    own_start = doc_starts(own, ends_ref)

    def step16(kb, state):
        m, l, acc = state
        kv = sp_ref[rows(kb, tile), 384:512]
        kpos = iota((tile, tile), 0) + kb * tile
        ok = (kpos <= own) & (kpos >= own_start)
        s = jnp.where(ok, dot_nt(kv, q16) * 0.125, NEG)
        mn = jnp.maximum(m, jnp.max(s, axis=0, keepdims=True))
        p = jnp.where(ok, jnp.exp(s - mn), 0.0)
        a = jnp.exp(m - mn)
        l = l * a + jnp.sum(p, axis=0, keepdims=True)
        acc = acc * a + dot(vt_scr[kb, 192:256, :], p.astype(BF))
        return mn, l, acc

    def query_block(qb, state16):
        state16 = step16(qb, state16)
        q = sp_ref[rows(qb, tile), 0:128]
        qs = [only_head(q, 0), only_head(q, 1)]
        qpos = iota((1, tile), 1) + qb * tile
        qstart = doc_starts(qpos, ends_ref)
        low = first_block(qb, tile, ends_ref)

        def step(n, state):
            kb = qb - n
            k = sp_ref[rows(kb, tile), 128:256]
            kpos = iota((tile, tile), 0) + kb * tile
            ok = (kpos <= qpos) & (kpos >= qstart)
            new = []
            for head in range(2):
                m, l, acc = state[head]
                s = jnp.where(ok, dot_nt(k, qs[head]) * 0.125, NEG)
                mn = jnp.maximum(m, jnp.max(s, axis=0, keepdims=True))
                p = jnp.exp(s - mn)
                a = jnp.exp(m - mn)
                l = l * a + jnp.sum(p, axis=0, keepdims=True)
                vt = vt_scr[kb, head * HEAD:(head + 1) * HEAD, :]
                acc = acc * a + dot(vt, p.astype(BF))
                new.append((mn, l, acc))
            return tuple(new)

        state = step(0, (start, start))
        state = lax.fori_loop(1, qb - low + 1, step, state)
        out = jnp.concatenate([state[0][2] / state[0][1], state[1][2] / state[1][1]], axis=0).T
        of_ref[rows(qb, tile), :] = out
        ob_scr[rows(qb, tile), :] = out.astype(BF)
        lse_ref[qb] = jnp.concatenate([s[0] + jnp.log(s[1]) for s in state], axis=0)
        return state16

    start = (jnp.full((1, tile), NEG, F32), jnp.zeros((1, tile), F32), jnp.zeros((HEAD, tile), F32))
    m, l, acc = lax.fori_loop(0, blocks, query_block, start)
    o16_ref[...] = jnp.concatenate([jnp.zeros_like(acc), acc / l], axis=0).T
    lse16_ref[...] = m + jnp.log(l)

    for b in range(blocks):
        pick = jnp.where(scol_ref[b * tile:(b + 1) * tile, :] == iota((tile, total), 1), 1.0, 0.0).astype(BF)
        shard = lax.rem(z + zs - b // 2, zs) * 2 + lax.rem(y + b % 2, 2)
        o_ref[shard] = dot(pick, ob_scr[...]).astype(BF)


def backward_kernel(
    ends_ref, w_ref, srow_ref, scol_ref, own_ref, sp_ref, kt_ref, of_ref, lse_ref,
    do_ref, q16_ref, do16_ref, o16_ref, lse16_ref,
    dp_ref, dq16_ref, *refs,
):
    total = sp_ref.shape[0]
    tile = own_ref.shape[1]
    blocks = total // tile
    dh_refs, (dos_scr, acc_scr, acc16_scr, dps_scr) = refs[:blocks], refs[blocks:]

    places = jnp.concatenate([srow_ref[b] for b in range(blocks)], axis=1)

    @pl.loop(0, blocks)
    def _(b):
        r = rows(b, tile)
        pick = jnp.where(places == iota((tile, total), 0) + b * tile, 1.0, 0.0).astype(BF)
        dos_scr[r, :] = dot(pick, do_ref[...]).astype(BF)
        acc_scr[r, :] = jnp.zeros((tile, 256), F32)

    own = own_ref[...]
    own_start = doc_starts(own, ends_ref)
    q16 = q16_ref[...]
    do16 = do16_ref[...]
    both = jnp.concatenate([q16, do16], axis=0)
    delta16 = jnp.sum((do16.astype(F32) * o16_ref[...]).T, axis=0, keepdims=True)
    lse16 = lse16_ref[...]

    def step16(kb, dq):
        kr = rows(kb, tile)
        kv = sp_ref[kr, 384:512]
        kpos = iota((tile, tile), 0) + kb * tile
        ok = (kpos <= own) & (kpos >= own_start)
        p = jnp.where(ok, jnp.exp(dot_nt(kv, q16) * 0.125 - lse16), 0.0)
        ds = (p * (dot_nt(kv, do16) - delta16)).astype(BF)
        acc16_scr[kr, :] = dot(jnp.concatenate([ds, p.astype(BF)], axis=1), both)
        return dq + dot_tn(ds, kv)

    def query_block(qb, dq16):
        dq16 = step16(qb, dq16)
        qr = rows(qb, tile)
        q = sp_ref[qr, 0:128]
        do = dos_scr[qr, :]
        qs = [only_head(q, 0), only_head(q, 1)]
        ds_ = [only_head(do, 0), only_head(do, 1)]
        q_two = jnp.concatenate(qs, axis=0)
        do_two = jnp.concatenate(ds_, axis=0)
        prod = (do.astype(F32) * of_ref[qr, :]).T
        delta = [jnp.sum(prod[:HEAD], axis=0, keepdims=True), jnp.sum(prod[HEAD:], axis=0, keepdims=True)]
        lse = lse_ref[qb]
        qpos = iota((1, tile), 1) + qb * tile
        qstart = doc_starts(qpos, ends_ref)
        low = first_block(qb, tile, ends_ref)

        def step(kb, dqt):
            kr = rows(kb, tile)
            k = sp_ref[kr, 128:256]
            v = sp_ref[kr, 256:384]
            kpos = iota((tile, tile), 0) + kb * tile
            ok = (kpos <= qpos) & (kpos >= qstart)
            ps, dss, new = [], [], []
            for head in range(2):
                s = dot_nt(k, qs[head]) * 0.125 - lse[head:head + 1]
                p = jnp.where(ok, jnp.exp(s), 0.0)
                dprob = dot_nt(v, ds_[head])
                ds = (p * (dprob - delta[head])).astype(BF)
                ps.append(p.astype(BF))
                dss.append(ds)
                new.append(dqt[head] + dot(kt_ref[kb, head * HEAD:(head + 1) * HEAD, :], ds))
            acc_scr[kr, 0:128] += dot(jnp.concatenate(dss, axis=1), q_two)
            acc_scr[kr, 128:256] += dot(jnp.concatenate(ps, axis=1), do_two)
            return tuple(new)

        zero = jnp.zeros((HEAD, tile), F32)
        dqt = lax.fori_loop(low, qb, step, step(qb, (zero, zero)))
        dps_scr[qr, 0:128] = (jnp.concatenate(dqt, axis=0).T * 0.125).astype(BF)
        return dq16

    dq16 = lax.fori_loop(0, blocks, query_block, jnp.zeros((tile, 128), F32))
    dq16 = (dq16 * 0.125).astype(BF)
    dq16_ref[...] = dq16

    @pl.loop(0, blocks)
    def _(b):
        r = rows(b, tile)
        dps_scr[r, 128:256] = (acc_scr[r, 0:128] * 0.125).astype(BF)
        dps_scr[r, 256:384] = acc_scr[r, 128:256].astype(BF)
        part = acc16_scr[r, :]
        dps_scr[r, 384:512] = jnp.where(iota(part.shape, 1) < HEAD, part * 0.125, part).astype(BF)

    for b in range(blocks):
        r = slice(b * tile, (b + 1) * tile)
        pick = jnp.where(scol_ref[r, :] == iota((tile, total), 1), 1.0, 0.0).astype(BF)
        dp = dot(pick, dps_scr[...]).astype(BF)
        dp_ref[r, :] = dp
        dh = dot_nt(dp, w_ref[:, :512])
        if b == 0:
            dh = dh + dot_nt(only_head(dq16, 0), w_ref[:, 512:640])
        dh_refs[b][...] = dh[:, :dh_refs[b].shape[1]].astype(BF)


def norm_stats(values):
    centre = values - jnp.mean(values, axis=-1, keepdims=True)
    spread = jnp.mean(centre * centre, axis=-1, keepdims=True)
    rate = lax.rsqrt(spread + 1e-05)
    return centre * rate, rate


def norm_back(grad, normed, rate, gain):
    scaled = grad * gain
    inner = jnp.mean(scaled * normed, axis=-1, keepdims=True)
    back = rate * (scaled - jnp.mean(scaled, axis=-1, keepdims=True) - normed * inner)
    return back, jnp.sum(grad * normed, axis=0, keepdims=True), jnp.sum(grad, axis=0, keepdims=True)


def put(ref, values):
    width = values.shape[1]
    ref[:, :width] = values
    ref[:, width:] = jnp.zeros((ref.shape[0], ref.shape[1] - width), ref.dtype)


def first_norm_kernel(tok_ref, slot_ref, gain_ref, bias_ref, h_ref):
    tile, feats = tok_ref.shape
    normed, _ = norm_stats(tok_ref[...].astype(F32))
    h_ref[:, :feats] = (normed * gain_ref[0:1] + bias_ref[0:1]).astype(BF)
    width = h_ref.shape[1] - feats
    slot = slot_ref[...]
    high = lax.shift_right_logical(slot, 6)
    lanes = iota((tile, width), 1)
    pair = jnp.where(lanes == 0, high, jnp.where(lanes == 1, slot - high * 64, 0))
    h_ref[:, feats:] = pair.astype(F32).astype(BF)


def slab(feats, n_shard, shard):
    mine = feats // HEAD // n_shard * HEAD
    spare = n_shard * mine
    left = feats - spare
    return [
        (shard * mine, mine), (feats + shard * mine, mine), (2 * feats + shard * mine, mine),
        (feats + spare, left), (2 * feats + spare, left), (spare, left),
    ]


def slab_part(feats, n_shard, shard, low, high):
    found, at = [], 0
    for start, width in slab(feats, n_shard, shard):
        first, end = max(at, low), min(at + width, high)
        if first < end:
            found.append((start + first - at, end - first, first - low))
        at = at + width
    return found


def in_width(feats, n_shard):
    return sum(width for _, width in slab(feats, n_shard, 0)) // 4


def pack_in_kernel(spot_ref, w_ref, out_w_ref, out_ref):
    feats = w_ref.shape[1] // 3
    n_shard = out_ref.shape[0]
    wide, out_wide = in_width(feats, n_shard), feats // 4
    for c in range(4):
        @pl.when(spot_ref[2] == c)
        def _(c=c):
            for s in range(n_shard):
                for column, width, place in slab_part(feats, n_shard, s, c * wide, (c + 1) * wide):
                    out_ref[s, :, place:place + width] = w_ref[:, column:column + width]
                out_ref[s, :, wide:wide + out_wide] = out_w_ref[:, c * out_wide:(c + 1) * out_wide]
                out_ref[s, :, wide + out_wide:] = jnp.zeros_like(out_ref[s, :, wide + out_wide:])


def pack_ff_kernel(n_shard, spot_ref, up_ref, down_ref, bias_ref, out_ref, own_bias_ref):
    feats = down_ref.shape[1]
    quarter = down_ref.shape[0] // 4
    aligned = -(-feats // 128) * 128
    out_ref[...] = jnp.zeros_like(out_ref)
    for c in range(4):
        r = (c % 2) * 2 + c // 2

        @pl.when(spot_ref[2] == c)
        def _(c=c, r=r):
            for s in range(n_shard):
                at = (s * 4 + r) * quarter
                out_ref[:, s * quarter:(s + 1) * quarter] = up_ref[:, at:at + quarter]
                own_bias_ref[:, s * quarter:(s + 1) * quarter] = bias_ref[:, at:at + quarter]
            out_ref[:, aligned:aligned + feats] = down_ref[r * quarter:(r + 1) * quarter, :]


def middle_kernel(
    spot_ref, o_ref, o16_ref, wa_ref, wb_ref, tok_ref, gain_ref, bias_ref,
    h_ref, middle_ref, attended_ref, w_ref,
):
    n_shard, tile, mine = o_ref.shape
    feats = tok_ref.shape[1]
    wide, first = feats // 4, in_width(feats, n_shard)
    for s in range(n_shard):
        attended_ref[:, s * mine:(s + 1) * mine] = o_ref[s]
    attended_ref[:, n_shard * mine:] = o16_ref[:, HEAD:].astype(BF)
    for c in range(4):
        @pl.when(spot_ref[2] == c)
        def _(c=c):
            for n, (ref, at) in enumerate(((wa_ref, 0), (wa_ref, 1), (wb_ref, 0), (wb_ref, 1))):
                place = c ^ n
                w_ref[:, place * wide:(place + 1) * wide] = ref[at, :, first:first + wide]
    middle = tok_ref[...].astype(F32) + (dot(attended_ref[...], w_ref[...]) + bias_ref[3:4])
    middle_ref[...] = middle
    normed, _ = norm_stats(middle)
    put(h_ref, (normed * gain_ref[1:2] + bias_ref[4:5]).astype(BF))


def by_corner(spot_ref, full_ref, wide, keep_a, keep_b, send_ref):
    for c in range(4):
        @pl.when(spot_ref[2] == c)
        def _(c=c):
            for n in range(4):
                p = c ^ n
                part = full_ref[:, p * wide:(p + 1) * wide]
                if n < 2:
                    put((keep_a, keep_b)[n], part)
                else:
                    put(send_ref.at[n - 2], part.astype(BF))


def middle_back_kernel(
    spot_ref, kept_ref, core_ref, far_ref, middle_ref, w_ref, cot_ref, attended_ref, gain_ref,
    dmiddle_ref, do_ref, do16_ref, keep_a, keep_b, send_ref, sums_ref, full_scr,
):
    n_shard, tile, mine = do_ref.shape
    feats = middle_ref.shape[1]
    dh = (kept_ref[...] + core_ref[...].astype(F32) + far_ref[...].astype(F32))[:, :feats]
    normed, rate = norm_stats(middle_ref[...])
    dout = cot_ref[:, :feats].astype(F32)
    back, gain_sum, bias_sum = norm_back(dh, normed, rate, gain_ref[1:2])
    dmiddle = dout + back
    dmiddle_ref[...] = dmiddle
    dbranch = dmiddle.astype(BF)
    dattended = dot_nt(dbranch, w_ref[...]).astype(BF)
    for s in range(n_shard):
        do_ref[s] = dattended[:, s * mine:(s + 1) * mine]
    last = dattended[:, n_shard * mine:]
    do16_ref[...] = jnp.concatenate([jnp.zeros_like(last), last], axis=1)
    full_scr[...] = dot_tn(attended_ref[...], dbranch)
    by_corner(spot_ref, full_scr, feats // 4, keep_a, keep_b, send_ref)
    sums_ref[0:1] = jnp.sum(dbranch.astype(F32), axis=0, keepdims=True)
    sums_ref[1:2] = bias_sum
    sums_ref[2:3] = jnp.sum(dout, axis=0, keepdims=True)
    sums_ref[3:4] = gain_sum


def last_kernel(kept_ref, y_ref, a_ref, b_ref, dmiddle_ref, tok_ref, gain_ref, out_ref, sums_ref):
    dh = kept_ref[...].astype(F32) + y_ref[...].astype(F32) + a_ref[...].astype(F32) + b_ref[...].astype(F32)
    dh = dh[:, :tok_ref.shape[1]]
    normed, rate = norm_stats(tok_ref[...].astype(F32))
    back, gain_sum, bias_sum = norm_back(dh, normed, rate, gain_ref[0:1])
    out_ref[...] = dmiddle_ref[...] + back
    sums_ref[0:1] = bias_sum
    sums_ref[1:2] = gain_sum


def feed_forward_kernel(
    h_a, h_b, h_c, g_a, g_b, g_c, w_ref, bias_ref,
    act_ref, dpre_ref, keep_a, keep_b, send_ref, sum_ref,
):
    tile, aligned = h_a.shape
    units, feats = act_ref.shape[1], w_ref.shape[0]
    total = jnp.zeros((1, units), F32)
    sources = ((h_a, g_a, None), (h_b, g_b, None), (h_c, g_c, 0), (h_c, g_c, 1))
    for n, (h_ref, g_ref, at) in enumerate(sources):
        h = h_ref[:, :feats] if at is None else h_ref[at, :, :feats]
        g = g_ref[:, :feats] if at is None else g_ref[at, :, :feats]
        r = slice(n * tile, (n + 1) * tile)
        pre = dot(h, w_ref[:, :units]) + bias_ref[...]
        dact = dot_nt(g, w_ref[:, aligned:aligned + feats])
        square = pre * pre
        root = 0.7978845608028654
        flat = jnp.tanh(root * pre * (1.0 + 0.044715 * square))
        half = 0.5 * (1.0 + flat)
        act_ref[r, :] = (pre * half).astype(BF)
        slope = half + 0.5 * pre * (1.0 - flat * flat) * root * (1.0 + 0.134145 * square)
        dpre = (dact * slope).astype(BF)
        dpre_ref[r, :] = dpre
        total = total + jnp.sum(dpre.astype(F32), axis=0, keepdims=True)
        dh = dot_nt(dpre, w_ref[:, :units])
        if n < 2:
            put((keep_a, keep_b)[n], dh)
        else:
            put(send_ref.at[n - 2], dh.astype(BF))
    sum_ref[...] = total


def feed_grads_kernel(
    h_a, h_b, h_c, g_a, g_b, g_c, w_ref, act_ref, dpre_ref,
    keep_a, keep_b, send_ref, grad_ref, h_scr, g_scr,
):
    tile, aligned = h_a.shape
    units, feats = act_ref.shape[1], w_ref.shape[0]
    down = w_ref[:, aligned:aligned + feats]
    sources = ((h_a, g_a, None), (h_b, g_b, None), (h_c, g_c, 0), (h_c, g_c, 1))
    for n, (h_ref, g_ref, at) in enumerate(sources):
        r = slice(n * tile, (n + 1) * tile)
        h_scr[r, :] = h_ref[:, :feats] if at is None else h_ref[at, :, :feats]
        g_scr[r, :] = g_ref[:, :feats] if at is None else g_ref[at, :, :feats]
    step = 256
    for at in range(0, units, step):
        c = slice(at, min(at + step, units))
        grad_ref[:, c] = dot_tn(h_scr[...], dpre_ref[:, c]).astype(BF)
    for at in range(0, feats, step):
        end = min(at + step, feats)
        part = dot_tn(act_ref[...], g_scr[:, at:end])
        grad_ref[:, aligned + at:aligned + end] = part.astype(BF)
    blank = jnp.zeros((grad_ref.shape[0], aligned - feats), BF)
    grad_ref[:, units:aligned] = blank
    grad_ref[:, aligned + feats:] = blank
    for n in range(4):
        mixed = dot(act_ref[n * tile:(n + 1) * tile, :], down)
        if n < 2:
            put((keep_a, keep_b)[n], mixed)
        else:
            put(send_ref.at[n - 2], mixed.astype(BF))


def in_grad_kernel(blocks, spot_ref, *refs):
    h_refs, (dp_ref, dq16_ref, keep_a, keep_b, send_ref, full_scr) = refs[:blocks], refs[blocks:]
    tile = dq16_ref.shape[0]
    feats = keep_a.shape[0]
    for at in range(0, 512, 256):
        acc = dot_tn(h_refs[0][:, :feats], dp_ref[:tile, at:at + 256])
        for b in range(1, blocks):
            acc = acc + dot_tn(h_refs[b][:, :feats], dp_ref[b * tile:(b + 1) * tile, at:at + 256])
        full_scr[:, at:at + 256] = acc
    full_scr[:, 512:576] = dot_tn(h_refs[0][:, :feats], dq16_ref[...])[:, :HEAD]
    by_corner(spot_ref, full_scr, in_width(feats, blocks), keep_a, keep_b, send_ref)


def join_kernel(wide, out_wide, a_ref, b_ref, c_ref, out_a_ref, out_b_ref, out_c_ref, to_ref):
    to_ref[...] = jnp.zeros_like(to_ref)
    part = a_ref[...] + b_ref[...].astype(F32) + c_ref[...].astype(F32)
    to_ref[:, :wide] = part[:, :wide].astype(BF)
    part = out_a_ref[...] + out_b_ref[...].astype(F32) + out_c_ref[...].astype(F32)
    to_ref[:, wide:wide + out_wide] = part[:, :out_wide].astype(BF)


def fold_kernel(wide, out_wide, in_ref, out_ref):
    n_shard = in_ref.shape[0]
    for s in range(n_shard):
        out_ref[:, s * wide:(s + 1) * wide] = in_ref[s, :, :wide]
    total = in_ref[0, :, wide:wide + out_wide].astype(F32)
    for s in range(1, n_shard):
        total = total + in_ref[s, :, wide:wide + out_wide].astype(F32)
    out_ref[:, n_shard * wide:n_shard * wide + out_wide] = total.astype(BF)
    out_ref[:, n_shard * wide + out_wide:] = jnp.zeros_like(out_ref[:, n_shard * wide + out_wide:])


def owned_kernel(n_shard, spot_ref, a_ref, b_ref, c_ref, up_ref, down_ref):
    quarter, feats = a_ref.shape[0], down_ref.shape[1]
    aligned = -(-feats // 128) * 128
    for c in range(4):
        @pl.when(spot_ref[2] == c)
        def _(c=c):
            for n, (ref, at) in enumerate(((a_ref, None), (b_ref, None), (c_ref, 0), (c_ref, 1))):
                place = c ^ n
                r = (place % 2) * 2 + place // 2
                part = ref[...] if at is None else ref[at]
                for s in range(n_shard):
                    to = (s * 4 + r) * quarter
                    up_ref[:, to:to + quarter] = part[:, s * quarter:(s + 1) * quarter].astype(F32)
                down_ref[r * quarter:(r + 1) * quarter, :] = part[:, aligned:aligned + feats].astype(F32)


def owned_in_kernel(n_shard, spot_ref, a_ref, b_ref, c_ref, out_ref, out_w_ref):
    feats = out_ref.shape[1] // 3
    wide, out_wide = in_width(feats, n_shard), feats // 4
    shared = 3 * (feats // HEAD // n_shard * HEAD)
    for c in range(4):
        @pl.when(spot_ref[2] == c)
        def _(c=c):
            for n, (ref, at) in enumerate(((a_ref, None), (b_ref, None), (c_ref, 0), (c_ref, 1))):
                place = c ^ n
                low = place * wide

                def block(s):
                    lanes = slice(s * wide, (s + 1) * wide)
                    return (ref[:, lanes] if at is None else ref[at, :, lanes]).astype(F32)

                lanes = slice(n_shard * wide, n_shard * wide + out_wide)
                part = ref[:, lanes] if at is None else ref[at, :, lanes]
                out_w_ref[:, place * out_wide:(place + 1) * out_wide] = part.astype(F32)
                for s in range(n_shard):
                    for column, width, to in slab_part(feats, n_shard, s, low, min(low + wide, shared)):
                        out_ref[:, column:column + width] = block(s)[:, to:to + width]
                if low + wide > shared:
                    total = block(0)
                    for s in range(1, n_shard):
                        total = total + block(s)
                    first = max(low, shared)
                    for column, width, to in slab_part(feats, n_shard, 0, first, low + wide):
                        to = to + first - low
                        out_ref[:, column:column + width] = total[:, to:to + width]


VM = pl.BlockSpec(memory_space=pltpu.VMEM)
SM = pl.BlockSpec(memory_space=pltpu.SMEM)


def run(kernel, outs, operands, scalars=0, scratch=(), size=58, flops=0.0):
    moved = sum(v.size * v.dtype.itemsize for v in operands)
    moved = moved + sum(math.prod(shape) * jnp.dtype(kind).itemsize for shape, kind in outs)
    return pl.pallas_call(
        kernel,
        out_shape=tuple(jax.ShapeDtypeStruct(shape, kind) for shape, kind in outs),
        in_specs=[SM] * scalars + [VM] * (len(operands) - scalars),
        out_specs=tuple([VM] * len(outs)),
        scratch_shapes=[pltpu.VMEM(shape, kind) for shape, kind in scratch],
        compiler_params=pltpu.CompilerParams(vmem_limit_bytes=size * 2**20),
        cost_estimate=pl.CostEstimate(flops=int(flops), bytes_accessed=int(moved), transcendentals=0),
    )(*operands)


def swap(values, axis):
    return lax.ppermute(values, axis, [(0, 1), (1, 0)])


def gather_rep(values):
    other = swap(values, "x")
    return values, other, swap(jnp.stack([values, other]), "core")


def scatter_rep(keep_a, keep_b, send):
    across = swap(send, "core")
    return keep_a, across[0], swap((keep_b + across[1].astype(F32)).astype(BF), "x")


def shift(values, step):
    size = lax.axis_size("z")
    return lax.ppermute(values, "z", [(n, (n + step) % size) for n in range(size)])


def together(*values):
    return lax.optimization_barrier(values)


def ring_gather(values, beside):
    size = lax.axis_size("z")
    column = [values] + [None] * (size - 1)
    other = [None] * size
    arrived, last = [(0, values)], {1: values, -1: values}
    for n in range(1, size // 2 + 2):
        places, moving = [], []
        for place, block in arrived:
            places.append((other, place))
            moving.append(swap(block, "y"))
        arrived = []
        if n <= size // 2:
            steps = (1, -1) if size - n > n else (1,)
            for step in steps:
                places.append((column, n if step == 1 else size - n))
                moving.append(shift(last[step], step))
        moving = beside(n, moving)
        for (target, place), block in zip(places, moving):
            target[place] = block
            if target is column:
                arrived.append((place, block))
                last[1 if place == n else -1] = block
    return [block for pair in zip(column, other) for block in pair]


def ring_scatter(parts, beside):
    size = lax.axis_size("z")
    kept, sent = parts[0::2], parts[1::2]
    half = size // 2
    joined, running = {}, {1: None, -1: None}
    wanted = [[half] + ([size - half + 1] if size - half + 1 < size else [])]
    wanted += [[n] + ([size - n + 1] if size - n + 1 < size else []) for n in range(half - 1, 0, -1)]
    wanted += [[0]]
    for index, now in enumerate(wanted + [[]]):
        moving = [swap(sent[n], "y") for n in now]
        steps = []
        if index > 0:
            n = half + 1 - index
            for step, place in ((-1, n), (1, size - n)):
                if n >= 1 and (step == -1 or size - n > n):
                    total = joined[place]
                    if running[step] is not None:
                        total = total + running[step].astype(F32)
                    steps.append(step)
                    moving.append(shift(total.astype(BF), step))
        if not moving:
            continue
        moving = beside(index + 1, moving)
        for n, block in zip(now, moving):
            joined[n] = block if n == 0 else kept[n].astype(F32) + block.astype(F32)
        for step, block in zip(steps, moving[len(now):]):
            running[step] = block
    return kept[0], joined[0], running[-1], running[1]


def sum_dp(values):
    if lax.axis_size("dp") > 1:
        return lax.psum(values, "dp")
    return values


def sum_all(values, beside):
    others = [shift(values, n) for n in range(1, lax.axis_size("z"))]
    for other in beside(1, others):
        values = values + other
    for n, axis in enumerate(("y", "core", "x")):
        (other,) = beside(n + 2, [swap(values, axis)])
        values = values + other
    return sum_dp(values)


def gather_shard(values):
    return lax.all_gather(values, SHARD, axis=0, tiled=True)


def scatter_shard(values):
    return lax.psum_scatter(values.astype(BF), SHARD, scatter_dimension=0, tiled=True)


def exchange_shard(values):
    return lax.all_to_all(values, SHARD, 0, 0, tiled=True)


def shards(
    tokens, slot, lengths, attn_in_weight, attn_out_weight, up_weight, down_weight,
    norm_gains, layer_biases, up_bias, cotangent,
):
    tile, feats = tokens.shape
    zs = lax.axis_size("z")
    n_shard = zs * 2
    total = n_shard * tile
    mine = feats // HEAD // n_shard * HEAD
    spare = n_shard * mine
    z, y = lax.axis_index("z"), lax.axis_index("y")
    me = z * 2 + y
    rep = lax.axis_index("x") * 2 + lax.axis_index("core")
    corner = lax.axis_index("core") * 2 + lax.axis_index("x")
    spot = jnp.stack([z, y, corner]).astype(jnp.int32)
    row_part = attn_in_weight.shape[0]
    ff_part = down_weight.shape[0]
    n_rep = 4
    quarter = ff_part // n_rep
    units = n_shard * quarter
    aligned = -(-feats // 128) * 128
    in_wide = in_width(feats, n_shard)
    out_wide = feats // n_rep
    both_wide = -(-(in_wide + out_wide) // 128) * 128
    in_full = -(-in_wide // 128) * 128
    out_full = -(-out_wide // 128) * 128
    both_wide = -(-(in_wide + out_wide) // 128) * 128
    fold_wide = -(-(n_shard * in_wide + out_wide) // 128) * 128

    ends = jnp.cumsum(lengths[0]).astype(jnp.int32)
    (h_first,) = run(
        first_norm_kernel, [((tile, aligned), BF)], (tokens, slot.reshape(tile, 1), norm_gains, layer_biases)
    )

    (in_pack,) = run(
        pack_in_kernel, [((n_shard, row_part, both_wide), BF)], (spot, attn_in_weight, attn_out_weight), 1
    )
    ff_pack, up_bias_mine = run(
        functools.partial(pack_ff_kernel, n_shard),
        [((row_part, 2 * aligned), BF), ((1, units), F32)],
        (spot, up_weight, down_weight, up_bias.reshape(1, -1)), 1,
    )
    held = dict(
        in_own=exchange_shard(in_pack).reshape(feats, both_wide),
        dout=jnp.pad(cotangent, ((0, 0), (0, aligned - feats))),
        ff_pack=ff_pack,
    )

    held["w_all"] = gather_shard(ff_pack)

    def beside_gather(n, moving):
        names = []
        if n == 1:
            held["dout_far"] = swap(held["dout"], "x")
            names = ["in_own", "dout", "dout_far"]
        elif n == 2:
            held["in_far"] = swap(held["in_own"], "x")
            names = ["in_own", "in_far", "dout", "dout_far"]
        elif n == 3:
            held["in_a"] = jnp.stack([held["in_own"], held["in_far"]])
            held["in_b"] = swap(held["in_a"], "core")
            held["g_core"] = swap(jnp.stack([held["dout"], held["dout_far"]]), "core")
            names = ["in_a", "in_b", "dout", "dout_far", "g_core"]
        *moving, = together(*moving, *[held[name] for name in names])
        for name in reversed(names):
            held[name] = moving.pop()
        return moving

    h_parts = ring_gather(h_first, beside_gather)
    w_all, in_a, in_b = held["w_all"], held["in_a"], held["in_b"]
    dout, g_rep = held["dout"], (held["dout"], held["dout_far"], held["g_core"])
    (sp, kt, o_own, of, lse, q16, o16, lse16, w_own, slot_rows, slot_columns) = run(
        functools.partial(forward_kernel, n_shard),
        [
            ((total, 512), BF), ((n_shard, 128, tile), BF), ((n_shard, tile, 128), BF), ((total, 128), F32),
            ((n_shard, 2, tile), F32), ((tile, 128), BF), ((tile, 128), F32), ((1, tile), F32),
            ((aligned, 640), BF), ((n_shard, 1, tile), jnp.int32), ((total, 1), jnp.int32),
        ],
        (ends, spot, *h_parts, in_a, in_b, layer_biases, slot.reshape(1, tile)), 2,
        scratch=[((total, 640), BF), ((n_shard, 256, tile), BF), ((total, 128), BF), ((1, total), jnp.int32)],
        size=58, flops=30e9,
    )
    o_back = exchange_shard(o_own)
    h_second, middle, attended, w_out = run(
        middle_kernel,
        [((tile, aligned), BF), ((tile, feats), F32), ((tile, feats), BF), ((feats, feats), BF)],
        (spot, o_back, o16, in_a, in_b, tokens, norm_gains, layer_biases), 1, flops=2e9,
    )

    h_rep = gather_rep(h_second)
    whole, one, pair = (n_rep * tile, units), (tile, aligned), (2, tile, aligned)
    act, dpre, *dh_terms, up_bias_grad = run(
        feed_forward_kernel,
        [(whole, BF), (whole, BF), (one, F32), (one, F32), (pair, BF), ((1, units), F32)],
        (*h_rep, *g_rep, w_all, up_bias_mine), flops=10e9,
    )
    kept, joined, send = dh_terms
    across = swap(send, "core")
    joined, act, dpre = together((joined + across[1].astype(F32)).astype(BF), act, dpre)
    *mixed_terms, ff_grads = run(
        feed_grads_kernel,
        [(one, F32), (one, F32), (pair, BF), ((feats, 2 * aligned), BF)],
        (*h_rep, *g_rep, w_all, act, dpre),
        scratch=[((n_rep * tile, feats), BF)] * 2, size=58, flops=10e9,
    )
    far, ff_grads = together(swap(joined, "x"), ff_grads)
    ff_owned = sum_dp(scatter_shard(ff_grads))
    dh_terms = (kept, across[0], far)
    dmiddle, do_all, do16, *out_terms, sums = run(
        middle_back_kernel,
        [
            ((tile, feats), F32), ((n_shard, tile, mine), BF), ((tile, 128), BF),
            ((feats, out_full), F32), ((feats, out_full), F32), ((2, feats, out_full), BF), ((4, feats), F32),
        ],
        (spot, *dh_terms, middle, w_out, dout, attended, norm_gains), 1,
        scratch=[((feats, feats), F32)], flops=3e9,
    )

    out_terms = scatter_rep(*out_terms)
    do_own, *out_terms = together(exchange_shard(do_all).reshape(total, mine), *out_terms)
    dp, dq16, *dh_parts = run(
        backward_kernel,
        [((total, 512), BF), ((tile, 128), BF)] + [((tile, aligned), BF)] * n_shard,
        (
            ends, w_own, slot_rows, slot_columns, slot.reshape(1, tile),
            sp, kt, of, lse, do_own, q16, do16, o16, lse16,
        ),
        1,
        scratch=[((total, 128), BF), ((total, 256), F32), ((total, 128), F32), ((total, 512), BF)],
        size=58, flops=30e9,
    )
    in_kept, in_joined, in_send = run(
        functools.partial(in_grad_kernel, n_shard),
        [((feats, in_full), F32), ((feats, in_full), F32), ((2, feats, in_full), BF)],
        (spot, *h_parts, dp, dq16), 1, scratch=[((feats, 576), F32)], flops=3e9,
    )

    def beside_scatter(n, moving):
        if n == 2:
            held["across"] = swap(in_send, "core")
            far = swap((in_joined + held["across"][1].astype(F32)).astype(BF), "x")
            *moving, held["far"] = together(*moving, far)
        elif n == 3:
            (grad,) = run(
                functools.partial(join_kernel, in_wide, out_wide),
                [((feats, both_wide), BF)],
                (in_kept, held["across"][0], held["far"], *out_terms),
            )
            in_back = exchange_shard(grad.reshape(n_shard, row_part, both_wide))
            ff_far = swap(ff_owned, "x")
            kept, joined, send = mixed_terms
            across = swap(send, "core")
            far = swap((joined + across[1].astype(F32)).astype(BF), "x")
            *moving, held["in_back"], held["ff"], held["ff_far"], far = together(
                *moving, in_back, ff_owned, ff_far, far
            )
            parts = kept + across[0].astype(F32) + far.astype(F32)
            held["mixed"] = (middle + parts[:, :feats] + layer_biases[5]).astype(BF)
        return moving

    dh_first = ring_scatter(dh_parts, beside_scatter)
    (in_back,) = run(
        functools.partial(fold_kernel, in_wide, out_wide), [((row_part, fold_wide), BF)], (held["in_back"],)
    )
    *dh_first, in_back = together(*dh_first, sum_dp(in_back))

    def beside_sum(n, moving):
        if n == 1:
            ff_core = swap(jnp.stack([held["ff"], held["ff_far"]]), "core")
            *moving, held["in_far"], held["ff_core"] = together(*moving, swap(in_back, "x"), ff_core)
        elif n == 2:
            in_core = swap(jnp.stack([in_back, held["in_far"]]), "core")
            up_out, down_out = run(
                functools.partial(owned_kernel, n_shard),
                [((row_part, up_weight.shape[1]), F32), ((ff_part, feats), F32)],
                (spot, held["ff"], held["ff_far"], held["ff_core"]), 1,
            )
            *moving, held["in_core"], held["up"], held["down"] = together(*moving, in_core, up_out, down_out)
        elif n == 4:
            in_out, out_out = run(
                functools.partial(owned_in_kernel, n_shard),
                [((row_part, 3 * feats), F32), ((row_part, feats), F32)],
                (spot, in_back, held["in_far"], held["in_core"]), 1,
            )
            *moving, held["in"], held["out"] = together(*moving, in_out, out_out)
        return moving

    tokens_grad, first_sums = run(
        last_kernel, [((tile, feats), F32), ((2, feats), F32)], (*dh_first, dmiddle, tokens, norm_gains)
    )

    zeros = functools.partial(jnp.zeros, dtype=F32)
    dp_sums = jnp.sum(dp.astype(F32), axis=0)
    query_sums = lax.dynamic_update_slice(zeros(feats), dp_sums[:mine], (me * mine,))
    query_sums = query_sums + jnp.pad(jnp.sum(dq16[:, :HEAD].astype(F32), axis=0), (spare, 0))
    value_sums = lax.dynamic_update_slice(zeros(feats), dp_sums[2 * mine : 3 * mine], (me * mine,))
    value_sums = value_sums + jnp.pad(dp_sums[3 * mine + HEAD : 3 * mine + 2 * HEAD], (spare, 0))
    place = (jnp.arange(n_rep) == rep)[:, None]
    vectors = jnp.concatenate(
        [
            first_sums[0:1], jnp.stack([query_sums, value_sums]), sums[0:3], first_sums[1:2], sums[3:4],
            jnp.where(place, up_bias_grad, 0.0),
        ]
    )
    vectors = lax.dynamic_slice_in_dim(sum_all(vectors, beside_sum), me * row_part, row_part, 1)

    return (
        held["mixed"], tokens_grad, held["in"], held["out"], held["up"], held["down"],
        vectors[6:8], vectors[0:6], vectors[8:].reshape(-1),
    )


def solution(mesh):
    replicas, n_shard = mesh.shape["replica"], mesh.shape["shard"]
    fine = Mesh(
        mesh.devices.reshape(replicas // 4, 2, 2, n_shard // 2, 2), ("dp", "x", "core", "z", "y")
    )
    rep = ("dp", "x", "core")
    both = rep + SHARD
    in_specs = (
        P(both, None), P(both), P(rep, None), P(SHARD, None), P(SHARD, None), P(SHARD, None), P(SHARD, None),
        P(), P(), P(), P(both, None),
    )
    out_specs = (
        P(both, None), P(both, None), P(SHARD, None), P(SHARD, None), P(SHARD, None), P(SHARD, None),
        P(None, SHARD), P(None, SHARD), P(SHARD),
    )
    return jax.shard_map(shards, mesh=fine, in_specs=in_specs, out_specs=out_specs, check_vma=False)
```

profile of v0, /device:TPU:0, one launch (start us, length us, event | category | flops | bytes accessed | tf_op | source)
XLA Modules:
  0.0 483.3 jit_solution(4203413687743073903)
XLA Ops:
  10.5 7.4 %all-to-all-start = ((bf16[8,136,512]{2,1,0:T(8,128)(2,1)}), bf16[8,136,512]{2,1,0:T(8,128)(2,1)S(1)}, u32[]{:S(2)}, u32[]{:S(2)}) async-start(bf16[8,136,512]{2,1,0:T(8,128)(2,1)} %shard_map.179), calls=%async_computation | async-start | bytes 2228224 | tf_op jit(solution)/shard_map/all_to_all | solution.py:705
  33.4 17.7 %collective-permute-done.2.refs_6_ = bf16[256,1152]{1,0:T(8,128)(2,1)S(1)} collective-permute-done((bf16[256,1152]{1,0:T(8,128)(2,1)}, bf16[256,1152]{1,0:T(8,128)(2,1)S(1)}, u32[]{:S(2)}, u32[]{:S(2)}) %collective-permute-start.2) | collective-permute-done | bytes 589856 | tf_op jit(solution)/shard_map/ppermute | solution.py:618
  51.0 14.6 %collective-permute-done.1.refs_2_ = bf16[256,1152]{1,0:T(8,128)(2,1)S(1)} collective-permute-done((bf16[256,1152]{1,0:T(8,128)(2,1)}, bf16[256,1152]{1,0:T(8,128)(2,1)S(1)}, u32[]{:S(2)}, u32[]{:S(2)}) %collective-permute-start.1) | collective-permute-done | bytes 589856 | tf_op jit(solution)/shard_map/ppermute | solution.py:618
  79.3 5.6 %collective-permute-done.5.refs_7_ = bf16[256,1152]{1,0:T(8,128)(2,1)} collective-permute-done((bf16[256,1152]{1,0:T(8,128)(2,1)}, bf16[256,1152]{1,0:T(8,128)(2,1)}, u32[]{:S(2)}, u32[]{:S(2)}) %collective-permute-start.5) | collective-permute-done | bytes 589856 | tf_op jit(solution)/shard_map/ppermute | solution.py:603
  89.3 12.7 %collective-permute-done.4.refs_3_ = bf16[256,1152]{1,0:T(8,128)(2,1)} collective-permute-done((bf16[256,1152]{1,0:T(8,128)(2,1)}, bf16[256,1152]{1,0:T(8,128)(2,1)}, u32[]{:S(2)}, u32[]{:S(2)}) %collective-permute-start.4) | collective-permute-done | bytes 589856 | tf_op jit(solution)/shard_map/ppermute | solution.py:603
  106.4 15.1 %collective-permute-done.8.refs_5_ = bf16[256,1152]{1,0:T(8,128)(2,1)S(1)} collective-permute-done((bf16[256,1152]{1,0:T(8,128)(2,1)}, bf16[256,1152]{1,0:T(8,128)(2,1)S(1)}, u32[]{:S(2)}, u32[]{:S(2)}) %collective-permute-start.8) | collective-permute-done | bytes 589856 | tf_op jit(solution)/shard_map/ppermute | solution.py:603
  122.3 34.1 %shard_map.180 = (bf16[2048,512]{1,0:T(8,128)(2,1)}, bf16[8,128,256]{2,1,0:T(8,128)(2,1)}, bf16[8,256,128]{2,1,0:T(8,128)(2,1)}, f32[2048,128]{1,0:T(8,128)}, f3...) custom-call(s32[6]{0:T(128)} %bitcast.71, ...), custom_call_target="tpu_custom_call" | custom-call | flops 30000001024 | bytes 15101476 | tf_op jit(solution)/shard_map/pallas_call | solution.py:591
  156.4 29.2 %all_to_all.20.o_ref = bf16[8,256,128]{2,1,0:T(8,128)(2,1)} all-to-all(bf16[8,256,128]{2,1,0:T(8,128)(2,1)} %get-tuple-element.133), channel_id=1, replica_groups=mesh['dp'=1,'x'=2,'core'=2,'z'=4,'y'=2] {'z','y'}, dimensions={0} | all-to-all | bytes 1048576 | tf_op jit(solution)/shard_map/all_to_all | solution.py:705
  185.6 6.5 %shard_map.181 = (bf16[256,1152]{1,0:T(8,128)(2,1)}, f32[256,1088]{1,0:T(8,128)}, bf16[256,1088]{1,0:T(8,128)(2,1)}, bf16[1088,1088]{1,0:T(8,128)(2,1)}) custom-call(s32[3]{0:T(128)} %pad_add_fusion.spot_ref, bf16[8,256,128]{2,1,0:T(8,128)(2,1)} %all_to_all.20.o_ref, f32[256,128]{1,0:T(8,128)} %get-tuple-element.134.o16_ref, ...), custom_call_target="tpu_custom_call" | custom-call | flops 2000000000 | bytes 10332172 | tf_op jit(solution)/shard_map/pallas_call | solution.py:591
  192.1 15.5 %collective-permute-done.11.h_b = bf16[256,1152]{1,0:T(8,128)(2,1)S(1)} collective-permute-done((bf16[256,1152]{1,0:T(8,128)(2,1)}, bf16[256,1152]{1,0:T(8,128)(2,1)S(1)}, u32[]{:S(2)}, u32[]{:S(2)}) %collective-permute-start.11) | collective-permute-done | bytes 589856 | tf_op jit(solution)/shard_map/ppermute | solution.py:603
  212.9 16.8 %shard_map.183 = (bf16[1024,1088]{1,0:T(8,128)(2,1)}, bf16[1024,1088]{1,0:T(8,128)(2,1)}, f32[256,1152]{1,0:T(8,128)}, f32[256,1152]{1,0:T(8,128)}, bf16[2,256,1152]{2,1,0:T(8,128)(2,1)}, /*index=5*/f32[1,1088]{1,0:T(1,128)}) custom-call(bf16[256,1152]{1,0:T(8,128)(2,1)} %get-tuple-element.136.h_a, bf16[256,1152]{1,0:T(8,128)(2,1)} %copy-done.19, ...), custom_call_target="tpu_custom_call" | custom-call | flops 10000000000 | bytes 17736192 | tf_op jit(solution)/shard_map/pallas_call | solution.py:591
  234.5 16.6 %shard_map.184 = (f32[256,1152]{1,0:T(8,128)}, f32[256,1152]{1,0:T(8,128)}, bf16[2,256,1152]{2,1,0:T(8,128)(2,1)}, bf16[1088,2304]{1,0:T(8,128)(2,1)}) custom-call(bf16[256,1152]{1,0:T(8,128)(2,1)} %get-tuple-element.136.h_a, bf16[256,1152]{1,0:T(8,128)(2,1)} %copy-done.19, bf16[2,256,1152]{2,1,0:T(8,128)(2,1)} %copy-done.28, bf16[256,1152]{1,0:T(8,128)(2,1)} %copy-done.4, ...), custom_call_target="tpu_custom_call" | custom-call | flops 10000000000 | bytes 22740992 | tf_op jit(solution)/shard_map/pallas_call | solution.py:591
  252.9 9.7 %shard_map.185 = (f32[256,1088]{1,0:T(8,128)}, bf16[8,256,128]{2,1,0:T(8,128)(2,1)}, bf16[256,128]{1,0:T(8,128)(2,1)}, f32[1088,384]{1,0:T(8,128)}, f32[1088,384...) custom-call(s32[3]{0:T(128)} %pad_add_fusion.spot_ref, f32[256,1152]{1,0:T(8,128)} %get-tuple-element.157.kept_ref, ...), custom_call_target="tpu_custom_call" | custom-call | flops 3000000000 | bytes 13731340 | tf_op jit(solution)/shard_map/pallas_call | solution.py:591
  271.2 24.5 %all-to-all-done.2 = bf16[8,256,128]{2,1,0:T(8,128)(2,1)} async-done(((bf16[8,256,128]{2,1,0:T(8,128)(2,1)}), bf16[8,256,128]{2,1,0:T(8,128)(2,1)}, u32[]{:S(2)}, u32[]{:S(2)}) %all-to-all-start.2) | async-done | bytes 524320 | tf_op jit(solution)/shard_map/all_to_all | solution.py:705
  295.7 33.7 %shard_map.186 = (bf16[2048,512]{1,0:T(8,128)(2,1)}, bf16[256,128]{1,0:T(8,128)(2,1)}, bf16[256,1152]{1,0:T(8,128)(2,1)}, bf16[256,1152]{1,0:T(8,128)(2,1)}, bf1...) custom-call(s32[6]{0:T(128)} %bitcast.72, ...), custom_call_target="tpu_custom_call" | custom-call | flops 30000001024 | bytes 12847128 | tf_op jit(solution)/shard_map/pallas_call | solution.py:591
  331.0 8.5 %shard_map.187 = (f32[1088,256]{1,0:T(8,128)}, f32[1088,256]{1,0:T(8,128)}, bf16[2,1088,256]{2,1,0:T(8,128)(2,1)}) custom-call(s32[3]{0:T(128)} %pad_add_fusion.spot_ref, bf16[256,1152]{1,0:T(8,128)(2,1)} %shard_map.178.refs_0_, bf16[256,1152]{1,0:T(8,128)(2,1)} %collective-permute-done.refs_1_, bf16[256,1152]{1,0:T(8,128)(2,1)} %copy-done.30, ...), custom_call_target="tpu_custom_call" | custom-call | flops 3000000000 | bytes 10223628 | tf_op jit(solution)/shard_map/pallas_call | solution.py:591
  346.3 11.3 %collective-permute-start.23 = (bf16[1088,256]{1,0:T(8,128)(2,1)S(1)}, bf16[1088,256]{1,0:T(8,128)(2,1)S(1)}, u32[]{:S(2)}, u32[]{:S(2)}) collective-permute-start(bf16[1088,256]{1,0:T(8,128)(2,1)S(1)} %fusion.7), channel_id=1, source_target_pairs={{0,16},{16,0},{1,17},{17,1},{2,18},{18,2},{3,19},{19,3},{4,20},{20... | collective-permute-start | bytes 1671176 | tf_op jit(solution)/shard_map/ppermute | solution.py:603
  362.6 7.0 %collective-permute-done.21 = bf16[256,1152]{1,0:T(8,128)(2,1)S(1)} collective-permute-done((bf16[256,1152]{1,0:T(8,128)(2,1)S(1)}, bf16[256,1152]{1,0:T(8,128)(2,1)S(1)}, u32[]{:S(2)}, u32[]{:S(2)}) %collective-permute-start.21) | collective-permute-done | bytes 589856 | tf_op jit(solution)/shard_map/ppermute | solution.py:618
  399.0 9.3 %collective-permute-done.18.y_ref = bf16[256,1152]{1,0:T(8,128)(2,1)} collective-permute-done((bf16[256,1152]{1,0:T(8,128)(2,1)}, bf16[256,1152]{1,0:T(8,128)(2,1)}, u32[]{:S(2)}, u32[]{:S(2)}) %collective-permute-start.18) | collective-permute-done | bytes 589856 | tf_op jit(solution)/shard_map/ppermute | solution.py:603
  408.4 6.3 %collective-permute-done.26.b_ref = bf16[256,1152]{1,0:T(8,128)(2,1)} collective-permute-done((bf16[256,1152]{1,0:T(8,128)(2,1)}, bf16[256,1152]{1,0:T(8,128)(2,1)}, u32[]{:S(2)}, u32[]{:S(2)}) %collective-permute-start.26) | collective-permute-done | bytes 589856 | tf_op jit(solution)/shard_map/ppermute | solution.py:618
  414.7 12.8 %collective-permute-done.24.a_ref = bf16[256,1152]{1,0:T(8,128)(2,1)} collective-permute-done((bf16[256,1152]{1,0:T(8,128)(2,1)}, bf16[256,1152]{1,0:T(8,128)(2,1)}, u32[]{:S(2)}, u32[]{:S(2)}) %collective-permute-start.24) | collective-permute-done | bytes 589856 | tf_op jit(solution)/shard_map/ppermute | solution.py:618
  439.7 7.3 %collective-permute-start.30 = (f32[12,1088]{1,0:T(8,128)S(1)}, f32[12,1088]{1,0:T(8,128)S(1)}, u32[]{:S(2)}, u32[]{:S(2)}) collective-permute-start(f32[12,1088]{1,0:T(8,128)S(1)} %concatenate.3), channel_id=1, source_target_pairs={{0,4},{2,6},{4,0},{6,2},{1,5},{3,7},{5,1},{7,3},{8,12},{10,14},{12... | collective-permute-start | bytes 156680 | tf_op jit(solution)/shard_map/ppermute | solution.py:618
  448.3 5.9 %collective-permute-done.30 = f32[12,1088]{1,0:T(8,128)S(1)} collective-permute-done((f32[12,1088]{1,0:T(8,128)S(1)}, f32[12,1088]{1,0:T(8,128)S(1)}, u32[]{:S(2)}, u32[]{:S(2)}) %collective-permute-start.30) | collective-permute-done | bytes 52256 | tf_op jit(solution)/shard_map/ppermute | solution.py:618
  457.0 6.3 %shard_map.191 = (f32[136,4352]{1,0:T(8,128)}, f32[544,1088]{1,0:T(8,128)}) custom-call(s32[3]{0:T(128)} %pad_add_fusion.spot_ref, bf16[136,2304]{1,0:T(8,128)(2,1)} %reduce-scatter.2.cloned.1.call-done.a_ref, bf16[136,2304]{1,0:T(8,128)(2,1)} %copy-done.3, bf16[2,136,2304]{2,1,0:T(8,128)(2,1)} %collective-permute-done.33.c_ref), custom_call_target="tpu_custom_call" | custom-call | bytes 7241740 | tf_op jit(solution)/shard_map/pallas_call | solution.py:591
  (201 shorter events, 134.1 us)
Async XLA Ops:
  10.5 56.0 %all-to-all-start = ((bf16[8,136,512]{2,1,0:T(8,128)(2,1)}), bf16[8,136,512]{2,1,0:T(8,128)(2,1)S(1)}, u32[]{:S(2)}, u32[]{:S(2)}) async-start(bf16[8,136,512]{2,1,0:T(8,128)(2,1)} %shard_map.179), calls=%async_computation | async-start | bytes 2228224 | tf_op jit(solution)/shard_map/all_to_all | solution.py:705
  18.0 194.0 %all-gather.2.cloned.1.call-start = ((), (), s32[]{:S(2)}) async-start(), calls=%async_computation.5 | async-start | bytes 5640192 | tf_op jit(solution)/shard_map/all_gather | solution.py:697
  25.4 25.7 %collective-permute-start.2 = (bf16[256,1152]{1,0:T(8,128)(2,1)}, bf16[256,1152]{1,0:T(8,128)(2,1)S(1)}, u32[]{:S(2)}, u32[]{:S(2)}) collective-permute-start(bf16[256,1152]{1,0:T(8,128)(2,1)} %shard_map.178.refs_0_), channel_id=1, source_target_pairs={{0,6},{2,0},{4,2},{6,4},{1,7},{3,1},{5,3},{7,5},{8,14},{10,8},{12,... | collective-permute-start | bytes 1769480 | tf_op jit(solution)/shard_map/ppermute | solution.py:618
  29.1 36.5 %collective-permute-start.1 = (bf16[256,1152]{1,0:T(8,128)(2,1)}, bf16[256,1152]{1,0:T(8,128)(2,1)S(1)}, u32[]{:S(2)}, u32[]{:S(2)}) collective-permute-start(bf16[256,1152]{1,0:T(8,128)(2,1)} %shard_map.178.refs_0_), channel_id=1, source_target_pairs={{0,2},{2,4},{4,6},{6,0},{1,3},{3,5},{5,7},{7,1},{8,10},{10,12},{12... | collective-permute-start | bytes 1769480 | tf_op jit(solution)/shard_map/ppermute | solution.py:618
  29.1 37.4 %collective-permute-start = (bf16[256,1152]{1,0:T(8,128)(2,1)}, bf16[256,1152]{1,0:T(8,128)(2,1)}, u32[]{:S(2)}, u32[]{:S(2)}) collective-permute-start(bf16[256,1152]{1,0:T(8,128)(2,1)} %shard_map.178.refs_0_), channel_id=1, source_target_pairs={{0,1},{1,0},{2,3},{3,2},{4,5},{5,4},{6,7},{7,6},{8,9},{9,8},{10,11... | collective-permute-start | bytes 1769480 | tf_op jit(solution)/shard_map/ppermute | solution.py:603
  66.5 35.5 %collective-permute-start.7 = (bf16[1088,512]{1,0:T(8,128)(2,1)S(1)}, bf16[1088,512]{1,0:T(8,128)(2,1)S(1)}, u32[]{:S(2)}, u32[]{:S(2)}) collective-permute-start(bf16[1088,512]{1,0:T(8,128)(2,1)S(1)} %bitcast.55), channel_id=1, source_target_pairs={{0,16},{16,0},{1,17},{17,1},{2,18},{18,2},{3,19},{19,3},{4,20},{20... | collective-permute-start | bytes 3342344 | tf_op jit(solution)/shard_map/ppermute | solution.py:603
  69.8 19.5 %collective-permute-start.6 = (bf16[256,1152]{1,0:T(8,128)(2,1)}, bf16[256,1152]{1,0:T(8,128)(2,1)}, u32[]{:S(2)}, u32[]{:S(2)}) collective-permute-start(bf16[256,1152]{1,0:T(8,128)(2,1)} %copy-done.30), channel_id=1, source_target_pairs={{0,2},{2,4},{4,6},{6,0},{1,3},{3,5},{5,7},{7,1},{8,10},{10,12},{12... | collective-permute-start | bytes 1769480 | tf_op jit(solution)/shard_map/ppermute | solution.py:618
  75.3 26.7 %collective-permute-start.4 = (bf16[256,1152]{1,0:T(8,128)(2,1)}, bf16[256,1152]{1,0:T(8,128)(2,1)}, u32[]{:S(2)}, u32[]{:S(2)}) collective-permute-start(bf16[256,1152]{1,0:T(8,128)(2,1)} %copy-done.30), channel_id=1, source_target_pairs={{0,1},{1,0},{2,3},{3,2},{4,5},{5,4},{6,7},{7,6},{8,9},{9,8},{10,11... | collective-permute-start | bytes 1769480 | tf_op jit(solution)/shard_map/ppermute | solution.py:603
  79.2 311.1 %reduce-scatter.2.cloned.1.call-start = ((), (), s32[]{:S(2)}) async-start(), calls=%async_computation.6 | async-start | bytes 5640192 | tf_op jit(solution)/shard_map/reduce_scatter | solution.py:701
  262.6 33.1 %all-to-all-start.2 = ((bf16[8,256,128]{2,1,0:T(8,128)(2,1)}), bf16[8,256,128]{2,1,0:T(8,128)(2,1)}, u32[]{:S(2)}, u32[]{:S(2)}) async-start(bf16[8,256,128]{2,1,0:T(8,128)(2,1)} %get-tuple-element.163), calls=%async_computation.2 | async-start | bytes 1048576 | tf_op jit(solution)/shard_map/all_to_all | solution.py:705
  268.4 27.3 %collective-permute-start.17 = (bf16[1088,384]{1,0:T(8,128)(2,1)S(1)}, bf16[1088,384]{1,0:T(8,128)(2,1)S(1)}, u32[]{:S(2)}, u32[]{:S(2)}) collective-permute-start(bf16[1088,384]{1,0:T(8,128)(2,1)S(1)} %fusion), channel_id=1, source_target_pairs={{0,16},{16,0},{1,17},{17,1},{2,18},{18,2},{3,19},{19,3},{4,20},{20... | collective-permute-start | bytes 2506760 | tf_op jit(solution)/shard_map/ppermute | solution.py:603
  343.3 36.5 %collective-permute-start.14 = (bf16[2,256,1152]{2,1,0:T(8,128)(2,1)}, bf16[2,256,1152]{2,1,0:T(8,128)(2,1)S(1)}, u32[]{:S(2)}, u32[]{:S(2)}) collective-permute-start(bf16[2,256,1152]{2,1,0:T(8,128)(2,1)} %get-tuple-element.149), channel_id=1, source_target_pairs={{0,8},{8,0},{1,9},{9,1},{2,10},{10,2},{3,11},{11,3},{4,12},{12,4},... | collective-permute-start | bytes 3538952 | tf_op jit(solution)/shard_map/ppermute | solution.py:603
  343.4 19.2 %collective-permute-start.19 = (bf16[256,1152]{1,0:T(8,128)(2,1)S(1)}, bf16[256,1152]{1,0:T(8,128)(2,1)S(1)}, u32[]{:S(2)}, u32[]{:S(2)}) collective-permute-start(bf16[256,1152]{1,0:T(8,128)(2,1)S(1)} %copy-done.32), channel_id=1, source_target_pairs={{0,1},{1,0},{2,3},{3,2},{4,5},{5,4},{6,7},{7,6},{8,9},{9,8},{10,11... | collective-permute-start | bytes 1769480 | tf_op jit(solution)/shard_map/ppermute | solution.py:603
  346.1 23.5 %collective-permute-start.21 = (bf16[256,1152]{1,0:T(8,128)(2,1)S(1)}, bf16[256,1152]{1,0:T(8,128)(2,1)S(1)}, u32[]{:S(2)}, u32[]{:S(2)}) collective-permute-start(bf16[256,1152]{1,0:T(8,128)(2,1)S(1)} %add_convert_fusion.2), channel_id=1, source_target_pairs={{0,6},{2,0},{4,2},{6,4},{1,7},{3,1},{5,3},{7,5},{8,14},{10,8},{12,... | collective-permute-start | bytes 1769480 | tf_op jit(solution)/shard_map/ppermute | solution.py:618
  346.3 24.0 %collective-permute-start.23 = (bf16[1088,256]{1,0:T(8,128)(2,1)S(1)}, bf16[1088,256]{1,0:T(8,128)(2,1)S(1)}, u32[]{:S(2)}, u32[]{:S(2)}) collective-permute-start(bf16[1088,256]{1,0:T(8,128)(2,1)S(1)} %fusion.7), channel_id=1, source_target_pairs={{0,16},{16,0},{1,17},{17,1},{2,18},{18,2},{3,19},{19,3},{4,20},{20... | collective-permute-start | bytes 1671176 | tf_op jit(solution)/shard_map/ppermute | solution.py:603
  357.6 29.3 %collective-permute-start.25 = (bf16[256,1152]{1,0:T(8,128)(2,1)}, bf16[256,1152]{1,0:T(8,128)(2,1)}, u32[]{:S(2)}, u32[]{:S(2)}) collective-permute-start(bf16[256,1152]{1,0:T(8,128)(2,1)} %get-tuple-element.183), channel_id=1, source_target_pairs={{0,1},{1,0},{2,3},{3,2},{4,5},{5,4},{6,7},{7,6},{8,9},{9,8},{10,11... | collective-permute-start | bytes 1769480 | tf_op jit(solution)/shard_map/ppermute | solution.py:603
  375.2 52.3 %all-to-all-start.3 = ((bf16[8,136,512]{2,1,0:T(8,128)(2,1)}), bf16[8,136,512]{2,1,0:T(8,128)(2,1)S(1)}, u32[]{:S(2)}, u32[]{:S(2)}) async-start(bf16[8,136,512]{2,1,0:T(8,128)(2,1)} %bitcast.54), calls=%async_computation.3 | async-start | bytes 2228224 | tf_op jit(solution)/shard_map/all_to_all | solution.py:705
  380.8 18.3 %collective-permute-start.28 = (bf16[256,1152]{1,0:T(8,128)(2,1)}, bf16[256,1152]{1,0:T(8,128)(2,1)}, u32[]{:S(2)}, u32[]{:S(2)}) collective-permute-start(bf16[256,1152]{1,0:T(8,128)(2,1)} %fusion.5), channel_id=1, source_target_pairs={{0,16},{16,0},{1,17},{17,1},{2,18},{18,2},{3,19},{19,3},{4,20},{20... | collective-permute-start | bytes 1769480 | tf_op jit(solution)/shard_map/ppermute | solution.py:603
  384.8 23.5 %collective-permute-start.18 = (bf16[256,1152]{1,0:T(8,128)(2,1)}, bf16[256,1152]{1,0:T(8,128)(2,1)}, u32[]{:S(2)}, u32[]{:S(2)}) collective-permute-start(bf16[256,1152]{1,0:T(8,128)(2,1)} %get-tuple-element.171), channel_id=1, source_target_pairs={{0,1},{1,0},{2,3},{3,2},{4,5},{5,4},{6,7},{7,6},{8,9},{9,8},{10,11... | collective-permute-start | bytes 1769480 | tf_op jit(solution)/shard_map/ppermute | solution.py:603
  388.8 25.8 %collective-permute-start.26 = (bf16[256,1152]{1,0:T(8,128)(2,1)}, bf16[256,1152]{1,0:T(8,128)(2,1)}, u32[]{:S(2)}, u32[]{:S(2)}) collective-permute-start(bf16[256,1152]{1,0:T(8,128)(2,1)} %add_convert_fusion), channel_id=1, source_target_pairs={{0,2},{2,4},{4,6},{6,0},{1,3},{3,5},{5,7},{7,1},{8,10},{10,12},{12... | collective-permute-start | bytes 1769480 | tf_op jit(solution)/shard_map/ppermute | solution.py:618
  390.3 37.2 %collective-permute-start.27 = (bf16[136,2304]{1,0:T(8,128)(2,1)}, bf16[136,2304]{1,0:T(8,128)(2,1)S(1)}, u32[]{:S(2)}, u32[]{:S(2)}) collective-permute-start(bf16[136,2304]{1,0:T(8,128)(2,1)} %reduce-scatter.2.cloned.1.call-done.a_ref), channel_id=1, source_target_pairs={{0,16},{16,0},{1,17},{17,1},{2,18},{18,2},{3,19},{19,3},{4,20},{20... | collective-permute-start | bytes 1880072 | tf_op jit(solution)/shard_map/ppermute | solution.py:603
  392.8 34.7 %collective-permute-start.24 = (bf16[256,1152]{1,0:T(8,128)(2,1)}, bf16[256,1152]{1,0:T(8,128)(2,1)}, u32[]{:S(2)}, u32[]{:S(2)}) collective-permute-start(bf16[256,1152]{1,0:T(8,128)(2,1)} %add_convert_fusion.1), channel_id=1, source_target_pairs={{0,6},{2,0},{4,2},{6,4},{1,7},{3,1},{5,3},{7,5},{8,14},{10,8},{12,... | collective-permute-start | bytes 1769480 | tf_op jit(solution)/shard_map/ppermute | solution.py:618
  429.1 25.1 %collective-permute-start.33 = (bf16[2,136,2304]{2,1,0:T(8,128)(2,1)}, bf16[2,136,2304]{2,1,0:T(8,128)(2,1)}, u32[]{:S(2)}, u32[]{:S(2)}) collective-permute-start(bf16[2,136,2304]{2,1,0:T(8,128)(2,1)} %pad_maximum_fusion.1), channel_id=1, source_target_pairs={{0,8},{8,0},{1,9},{9,1},{2,10},{10,2},{3,11},{11,3},{4,12},{12,4},... | collective-permute-start | bytes 3760136 | tf_op jit(solution)/shard_map/ppermute | solution.py:603
  433.4 20.9 %collective-permute-start.32 = (bf16[136,1536]{1,0:T(8,128)(2,1)}, bf16[136,1536]{1,0:T(8,128)(2,1)S(1)}, u32[]{:S(2)}, u32[]{:S(2)}) collective-permute-start(bf16[136,1536]{1,0:T(8,128)(2,1)} %shard_map.189.a_ref), channel_id=1, source_target_pairs={{0,16},{16,0},{1,17},{17,1},{2,18},{18,2},{3,19},{19,3},{4,20},{20... | collective-permute-start | bytes 1253384 | tf_op jit(solution)/shard_map/ppermute | solution.py:603
  (54 other events, 683.9 us)
Sparse Core Ops, SparseCore 0:
  79.4 88.2 all-gather.1
  251.3 119.1 reduce-scatter.1
where the time goes:
time: 486 us; the launch traced here: 483 us
  waiting for transfers between devices  170 us (35%)
  Pallas kernels  155 us (32%)
  starting transfers between devices  77.3 us (16%)
  blocking collectives  29.2 us (6%)
  local copies, waits for them, and re-layouts  18.7 us (4%)
  other arithmetic  18.5 us (4%)
  between operations  14.7 us (3%)
    pallas_call x15, Pallas kernels, run(): pl.pallas_call(kernel, out_shape=tuple((jax.ShapeDtypeStruct(shape, kind)...  155 us
    ppermute x29, waiting for transfers between devices, swap(): return lax.ppermute(values, axis, [(0, 1), (1, 0)])  75.4 us
    ppermute x9, waiting for transfers between devices, shift(): lax.ppermute(values, 'z', [(n, (n + step) % size) for n in range(size)])  70 us
    ppermute x29, starting transfers between devices, swap(): return lax.ppermute(values, axis, [(0, 1), (1, 0)])  39.4 us
    all_to_all x1, blocking collectives, exchange_shard(): return lax.all_to_all(values, SHARD, 0, 0, tiled=True)  29.2 us
    all_to_all x3, waiting for transfers between devices, exchange_shard(): return lax.all_to_all(values, SHARD, 0, 0, tiled=True)  24.5 us
    ppermute x9, starting transfers between devices, shift(): lax.ppermute(values, 'z', [(n, (n + step) % size) for n in range(size)])  21.6 us
    all_to_all x3, starting transfers between devices, exchange_shard(): return lax.all_to_all(values, SHARD, 0, 0, tiled=True)  16.2 us
  transfers between devices with their start and end apart: 43, of which 22 were waited for; matrix products, arithmetic and copies ran while one was open for 5% of the time, Pallas kernels for 28%

commit v1 on v0

--- a/solution.py
+++ b/solution.py
@@ -441,15 +441,15 @@
 
 
 def feed_forward_kernel(
-    h_a, h_b, h_c, g_a, g_b, g_c, w_ref, bias_ref,
+    h_a, h_b, h_c, h_d, g_a, g_b, g_c, w_ref, bias_ref,
     act_ref, dpre_ref, keep_a, keep_b, send_ref, sum_ref,
 ):
     tile, aligned = h_a.shape
     units, feats = act_ref.shape[1], w_ref.shape[0]
     total = jnp.zeros((1, units), F32)
-    sources = ((h_a, g_a, None), (h_b, g_b, None), (h_c, g_c, 0), (h_c, g_c, 1))
+    sources = ((h_a, g_a, None), (h_b, g_b, None), (h_c, g_c, 0), (h_d, g_c, 1))
     for n, (h_ref, g_ref, at) in enumerate(sources):
-        h = h_ref[:, :feats] if at is None else h_ref[at, :, :feats]
+        h = h_ref[:, :feats]
         g = g_ref[:, :feats] if at is None else g_ref[at, :, :feats]
         r = slice(n * tile, (n + 1) * tile)
         pre = dot(h, w_ref[:, :units]) + bias_ref[...]
@@ -472,16 +472,16 @@
 
 
 def feed_grads_kernel(
-    h_a, h_b, h_c, g_a, g_b, g_c, w_ref, act_ref, dpre_ref,
+    h_a, h_b, h_c, h_d, g_a, g_b, g_c, w_ref, act_ref, dpre_ref,
     keep_a, keep_b, send_ref, grad_ref, h_scr, g_scr,
 ):
     tile, aligned = h_a.shape
     units, feats = act_ref.shape[1], w_ref.shape[0]
     down = w_ref[:, aligned:aligned + feats]
-    sources = ((h_a, g_a, None), (h_b, g_b, None), (h_c, g_c, 0), (h_c, g_c, 1))
+    sources = ((h_a, g_a, None), (h_b, g_b, None), (h_c, g_c, 0), (h_d, g_c, 1))
     for n, (h_ref, g_ref, at) in enumerate(sources):
         r = slice(n * tile, (n + 1) * tile)
-        h_scr[r, :] = h_ref[:, :feats] if at is None else h_ref[at, :, :feats]
+        h_scr[r, :] = h_ref[:, :feats]
         g_scr[r, :] = g_ref[:, :feats] if at is None else g_ref[at, :, :feats]
     step = 256
     for at in range(0, units, step):
@@ -605,7 +605,7 @@
 
 def gather_rep(values):
     other = swap(values, "x")
-    return values, other, swap(jnp.stack([values, other]), "core")
+    return values, other, swap(values, "core"), swap(other, "core")
 
 
 def scatter_rep(keep_a, keep_b, send):

time: 486 us -> 522 us (1.074)
  starting transfers between devices: 77.3 us -> 102 us
  waiting for transfers between devices: 170 us -> 185 us
  blocking collectives: 29.2 us -> 22.6 us
  Pallas kernels: 155 us -> 161 us
    ppermute x9, starting transfers between devices: 21.6 us -> 45.1 us  [shift(): lax.ppermute(values, 'z', [(n, (n + step) % size) for n in range(size)])]
    ppermute x9, waiting for transfers between devices: 70 us -> 92.3 us  [shift(): lax.ppermute(values, 'z', [(n, (n + step) % size) for n in range(size)])]
    ppermute x29 -> x30, waiting for transfers between devices: 75.4 us -> 67.7 us  [swap(): return lax.ppermute(values, axis, [(0, 1), (1, 0)])]
    all_to_all x1, blocking collectives: 29.2 us -> 22.6 us  [exchange_shard(): return lax.all_to_all(values, SHARD, 0, 0, tiled=True)]
    pallas_call x15, Pallas kernels: 155 us -> 161 us  [run(): pl.pallas_call(kernel, out_shape=tuple((jax.ShapeDtypeStruct(shape, kind)...]
    ppermute x29 -> x30, starting transfers between devices: 39.4 us -> 40.4 us  [swap(): return lax.ppermute(values, axis, [(0, 1), (1, 0)])]
  transfers between devices with their start and end apart: 43 -> 44, of which waited for: 22 -> 20; matrix products, arithmetic and copies ran while one was open for 5% -> 5% of each run, Pallas kernels for 28% -> 27%
where the time goes in v1:
time: 522 us; the launch traced here: 520 us
  waiting for transfers between devices  185 us (35%)
  Pallas kernels  161 us (31%)
  starting transfers between devices  102 us (20%)
  blocking collectives  22.6 us (4%)
  local copies, waits for them, and re-layouts  17.4 us (3%)
  other arithmetic  17.2 us (3%)
  between operations  14.7 us (3%)
    pallas_call x15, Pallas kernels, run(): pl.pallas_call(kernel, out_shape=tuple((jax.ShapeDtypeStruct(shape, kind)...  161 us
    ppermute x9, waiting for transfers between devices, shift(): lax.ppermute(values, 'z', [(n, (n + step) % size) for n in range(size)])  92.3 us
    ppermute x30, waiting for transfers between devices, swap(): return lax.ppermute(values, axis, [(0, 1), (1, 0)])  67.7 us
    ppermute x9, starting transfers between devices, shift(): lax.ppermute(values, 'z', [(n, (n + step) % size) for n in range(size)])  45.1 us
    ppermute x30, starting transfers between devices, swap(): return lax.ppermute(values, axis, [(0, 1), (1, 0)])  40.4 us
    all_to_all x3, waiting for transfers between devices, exchange_shard(): return lax.all_to_all(values, SHARD, 0, 0, tiled=True)  25.3 us
    all_to_all x1, blocking collectives, exchange_shard(): return lax.all_to_all(values, SHARD, 0, 0, tiled=True)  22.6 us
    all_to_all x3, starting transfers between devices, exchange_shard(): return lax.all_to_all(values, SHARD, 0, 0, tiled=True)  16.1 us
  transfers between devices with their start and end apart: 44, of which 20 were waited for; matrix products, arithmetic and copies ran while one was open for 5% of the time, Pallas kernels for 27%

profile of v1, /device:TPU:0, one launch (start us, length us, event | category | flops | bytes accessed | tf_op | source)
XLA Modules:
  0.0 519.8 jit_solution(15011399360527414465)
XLA Ops:
  10.6 7.4 %all-to-all-start = ((bf16[8,136,512]{2,1,0:T(8,128)(2,1)}), bf16[8,136,512]{2,1,0:T(8,128)(2,1)S(1)}, u32[]{:S(2)}, u32[]{:S(2)}) async-start(bf16[8,136,512]{2,1,0:T(8,128)(2,1)} %shard_map.179), calls=%async_computation | async-start | bytes 2228224 | tf_op jit(solution)/shard_map/all_to_all | solution.py:705
  33.4 37.0 %collective-permute-done.2.refs_6_ = bf16[256,1152]{1,0:T(8,128)(2,1)S(1)} collective-permute-done((bf16[256,1152]{1,0:T(8,128)(2,1)}, bf16[256,1152]{1,0:T(8,128)(2,1)S(1)}, u32[]{:S(2)}, u32[]{:S(2)}) %collective-permute-start.2) | collective-permute-done | bytes 589856 | tf_op jit(solution)/shard_map/ppermute | solution.py:618
  70.4 11.9 %collective-permute-done.1.refs_2_ = bf16[256,1152]{1,0:T(8,128)(2,1)S(1)} collective-permute-done((bf16[256,1152]{1,0:T(8,128)(2,1)}, bf16[256,1152]{1,0:T(8,128)(2,1)S(1)}, u32[]{:S(2)}, u32[]{:S(2)}) %collective-permute-start.1) | collective-permute-done | bytes 589856 | tf_op jit(solution)/shard_map/ppermute | solution.py:618
  89.0 28.1 %collective-permute-start.6 = (bf16[256,1152]{1,0:T(8,128)(2,1)S(1)}, bf16[256,1152]{1,0:T(8,128)(2,1)}, u32[]{:S(2)}, u32[]{:S(2)}) collective-permute-start(bf16[256,1152]{1,0:T(8,128)(2,1)S(1)} %collective-permute-done.1.refs_2_), channel_id=1, source_target_pairs={{0,2},{2,4},{4,6},{6,0},{1,3},{3,5},{5,7},{7,1},{8,10},{10,12},{12... | collective-permute-start | bytes 1769480 | tf_op jit(solution)/shard_map/ppermute | solution.py:618
  117.1 13.6 %collective-permute-done.6.refs_4_ = bf16[256,1152]{1,0:T(8,128)(2,1)} collective-permute-done((bf16[256,1152]{1,0:T(8,128)(2,1)S(1)}, bf16[256,1152]{1,0:T(8,128)(2,1)}, u32[]{:S(2)}, u32[]{:S(2)}) %collective-permute-start.6) | collective-permute-done | bytes 589856 | tf_op jit(solution)/shard_map/ppermute | solution.py:618
  130.6 8.9 %collective-permute-done.4.refs_3_ = bf16[256,1152]{1,0:T(8,128)(2,1)S(1)} collective-permute-done((bf16[256,1152]{1,0:T(8,128)(2,1)S(1)}, bf16[256,1152]{1,0:T(8,128)(2,1)S(1)}, u32[]{:S(2)}, u32[]{:S(2)}) %collective-permute-start.4) | collective-permute-done | bytes 589856 | tf_op jit(solution)/shard_map/ppermute | solution.py:603
  145.1 13.0 %collective-permute-done.8.refs_5_ = bf16[256,1152]{1,0:T(8,128)(2,1)S(1)} collective-permute-done((bf16[256,1152]{1,0:T(8,128)(2,1)}, bf16[256,1152]{1,0:T(8,128)(2,1)S(1)}, u32[]{:S(2)}, u32[]{:S(2)}) %collective-permute-start.8) | collective-permute-done | bytes 589856 | tf_op jit(solution)/shard_map/ppermute | solution.py:603
  159.0 37.0 %shard_map.180 = (bf16[2048,512]{1,0:T(8,128)(2,1)}, bf16[8,128,256]{2,1,0:T(8,128)(2,1)}, bf16[8,256,128]{2,1,0:T(8,128)(2,1)}, f32[2048,128]{1,0:T(8,128)}, f3...) custom-call(s32[6]{0:T(128)} %bitcast.67, ...), custom_call_target="tpu_custom_call" | custom-call | flops 30000001024 | bytes 15101476 | tf_op jit(solution)/shard_map/pallas_call | solution.py:591
  195.9 22.6 %all_to_all.20.o_ref = bf16[8,256,128]{2,1,0:T(8,128)(2,1)} all-to-all(bf16[8,256,128]{2,1,0:T(8,128)(2,1)} %get-tuple-element.133), channel_id=1, replica_groups=mesh['dp'=1,'x'=2,'core'=2,'z'=4,'y'=2] {'z','y'}, dimensions={0} | all-to-all | bytes 1048576 | tf_op jit(solution)/shard_map/all_to_all | solution.py:705
  218.5 6.5 %shard_map.181 = (bf16[256,1152]{1,0:T(8,128)(2,1)}, f32[256,1088]{1,0:T(8,128)}, bf16[256,1088]{1,0:T(8,128)(2,1)}, bf16[1088,1088]{1,0:T(8,128)(2,1)}) custom-call(s32[3]{0:T(128)} %pad_add_fusion.spot_ref, bf16[8,256,128]{2,1,0:T(8,128)(2,1)} %all_to_all.20.o_ref, f32[256,128]{1,0:T(8,128)} %get-tuple-element.134.o16_ref, ...), custom_call_target="tpu_custom_call" | custom-call | flops 2000000000 | bytes 10332172 | tf_op jit(solution)/shard_map/pallas_call | solution.py:591
  228.6 12.3 %collective-permute-done.11.h_b = bf16[256,1152]{1,0:T(8,128)(2,1)S(1)} collective-permute-done((bf16[256,1152]{1,0:T(8,128)(2,1)}, bf16[256,1152]{1,0:T(8,128)(2,1)S(1)}, u32[]{:S(2)}, u32[]{:S(2)}) %collective-permute-start.11) | collective-permute-done | bytes 589856 | tf_op jit(solution)/shard_map/ppermute | solution.py:603
  243.8 16.7 %shard_map.183 = (bf16[1024,1088]{1,0:T(8,128)(2,1)}, bf16[1024,1088]{1,0:T(8,128)(2,1)}, f32[256,1152]{1,0:T(8,128)}, f32[256,1152]{1,0:T(8,128)}, bf16[2,256,1152]{2,1,0:T(8,128)(2,1)}, /*index=5*/f32[1,1088]{1,0:T(1,128)}) custom-call(bf16[256,1152]{1,0:T(8,128)(2,1)} %get-tuple-element.136.h_a, bf16[256,1152]{1,0:T(8,128)(2,1)} %copy-done.34, ...), custom_call_target="tpu_custom_call" | custom-call | flops 10000000000 | bytes 17736192 | tf_op jit(solution)/shard_map/pallas_call | solution.py:591
  266.7 16.5 %shard_map.184 = (f32[256,1152]{1,0:T(8,128)}, f32[256,1152]{1,0:T(8,128)}, bf16[2,256,1152]{2,1,0:T(8,128)(2,1)}, bf16[1088,2304]{1,0:T(8,128)(2,1)}) custom-call(bf16[256,1152]{1,0:T(8,128)(2,1)} %get-tuple-element.136.h_a, bf16[256,1152]{1,0:T(8,128)(2,1)} %copy-done.34, bf16[256,1152]{1,0:T(8,128)(2,1)} %copy-done.35, bf16[256,1152]{1,0:T(8,128)(2,1)} %copy-done.36, ...), custom_call_target="tpu_custom_call" | custom-call | flops 10000000000 | bytes 22740992 | tf_op jit(solution)/shard_map/pallas_call | solution.py:591
  284.9 9.7 %shard_map.185 = (f32[256,1088]{1,0:T(8,128)}, bf16[8,256,128]{2,1,0:T(8,128)(2,1)}, bf16[256,128]{1,0:T(8,128)(2,1)}, f32[1088,384]{1,0:T(8,128)}, f32[1088,384...) custom-call(s32[3]{0:T(128)} %pad_add_fusion.spot_ref, f32[256,1152]{1,0:T(8,128)} %get-tuple-element.157.kept_ref, ...), custom_call_target="tpu_custom_call" | custom-call | flops 3000000000 | bytes 13731340 | tf_op jit(solution)/shard_map/pallas_call | solution.py:591
  301.8 25.3 %all-to-all-done.2 = bf16[8,256,128]{2,1,0:T(8,128)(2,1)} async-done(((bf16[8,256,128]{2,1,0:T(8,128)(2,1)}), bf16[8,256,128]{2,1,0:T(8,128)(2,1)}, u32[]{:S(2)}, u32[]{:S(2)}) %all-to-all-start.2) | async-done | bytes 524320 | tf_op jit(solution)/shard_map/all_to_all | solution.py:705
  327.1 36.9 %shard_map.186 = (bf16[2048,512]{1,0:T(8,128)(2,1)}, bf16[256,128]{1,0:T(8,128)(2,1)}, bf16[256,1152]{1,0:T(8,128)(2,1)}, bf16[256,1152]{1,0:T(8,128)(2,1)}, bf1...) custom-call(s32[6]{0:T(128)} %bitcast.68, ...), custom_call_target="tpu_custom_call" | custom-call | flops 30000001024 | bytes 12847128 | tf_op jit(solution)/shard_map/pallas_call | solution.py:591
  365.5 8.5 %shard_map.187 = (f32[1088,256]{1,0:T(8,128)}, f32[1088,256]{1,0:T(8,128)}, bf16[2,1088,256]{2,1,0:T(8,128)(2,1)}) custom-call(s32[3]{0:T(128)} %pad_add_fusion.spot_ref, bf16[256,1152]{1,0:T(8,128)(2,1)} %shard_map.178.refs_0_, bf16[256,1152]{1,0:T(8,128)(2,1)} %collective-permute-done.refs_1_, bf16[256,1152]{1,0:T(8,128)(2,1)} %copy-done.29, ...), custom_call_target="tpu_custom_call" | custom-call | flops 3000000000 | bytes 10223628 | tf_op jit(solution)/shard_map/pallas_call | solution.py:591
  375.1 11.8 %collective-permute-done.21 = bf16[256,1152]{1,0:T(8,128)(2,1)S(1)} collective-permute-done((bf16[256,1152]{1,0:T(8,128)(2,1)}, bf16[256,1152]{1,0:T(8,128)(2,1)S(1)}, u32[]{:S(2)}, u32[]{:S(2)}) %collective-permute-start.21) | collective-permute-done | bytes 589856 | tf_op jit(solution)/shard_map/ppermute | solution.py:603
  391.2 8.4 %collective-permute-done.20 = bf16[256,1152]{1,0:T(8,128)(2,1)S(1)} collective-permute-done((bf16[256,1152]{1,0:T(8,128)(2,1)S(1)}, bf16[256,1152]{1,0:T(8,128)(2,1)S(1)}, u32[]{:S(2)}, u32[]{:S(2)}) %collective-permute-start.20) | collective-permute-done | bytes 589856 | tf_op jit(solution)/shard_map/ppermute | solution.py:603
  438.8 9.0 %collective-permute-done.27.b_ref = bf16[256,1152]{1,0:T(8,128)(2,1)} collective-permute-done((bf16[256,1152]{1,0:T(8,128)(2,1)}, bf16[256,1152]{1,0:T(8,128)(2,1)}, u32[]{:S(2)}, u32[]{:S(2)}) %collective-permute-start.27) | collective-permute-done | bytes 589856 | tf_op jit(solution)/shard_map/ppermute | solution.py:618
  447.8 9.4 %collective-permute-done.25.a_ref = bf16[256,1152]{1,0:T(8,128)(2,1)} collective-permute-done((bf16[256,1152]{1,0:T(8,128)(2,1)}, bf16[256,1152]{1,0:T(8,128)(2,1)}, u32[]{:S(2)}, u32[]{:S(2)}) %collective-permute-start.25) | collective-permute-done | bytes 589856 | tf_op jit(solution)/shard_map/ppermute | solution.py:618
  463.0 7.5 %collective-permute-start.33 = (bf16[136,1536]{1,0:T(8,128)(2,1)}, bf16[136,1536]{1,0:T(8,128)(2,1)S(1)}, u32[]{:S(2)}, u32[]{:S(2)}) collective-permute-start(bf16[136,1536]{1,0:T(8,128)(2,1)} %shard_map.189.a_ref), channel_id=1, source_target_pairs={{0,16},{16,0},{1,17},{17,1},{2,18},{18,2},{3,19},{19,3},{4,20},{20... | collective-permute-start | bytes 1253384 | tf_op jit(solution)/shard_map/ppermute | solution.py:603
  478.0 6.9 %collective-permute-start.31 = (f32[12,1088]{1,0:T(8,128)S(1)}, f32[12,1088]{1,0:T(8,128)S(1)}, u32[]{:S(2)}, u32[]{:S(2)}) collective-permute-start(f32[12,1088]{1,0:T(8,128)S(1)} %concatenate.3), channel_id=1, source_target_pairs={{0,4},{2,6},{4,0},{6,2},{1,5},{3,7},{5,1},{7,3},{8,12},{10,14},{12... | collective-permute-start | bytes 156680 | tf_op jit(solution)/shard_map/ppermute | solution.py:618
  494.9 6.3 %shard_map.191 = (f32[136,4352]{1,0:T(8,128)}, f32[544,1088]{1,0:T(8,128)}) custom-call(s32[3]{0:T(128)} %pad_add_fusion.spot_ref, bf16[136,2304]{1,0:T(8,128)(2,1)} %reduce-scatter.2.cloned.1.call-done.a_ref, bf16[136,2304]{1,0:T(8,128)(2,1)} %copy-done.3, bf16[2,136,2304]{2,1,0:T(8,128)(2,1)} %collective-permute-done.34.c_ref), custom_call_target="tpu_custom_call" | custom-call | bytes 7241740 | tf_op jit(solution)/shard_map/pallas_call | solution.py:591
  (210 shorter events, 134.0 us)
Async XLA Ops:
  10.6 71.8 %all-to-all-start = ((bf16[8,136,512]{2,1,0:T(8,128)(2,1)}), bf16[8,136,512]{2,1,0:T(8,128)(2,1)S(1)}, u32[]{:S(2)}, u32[]{:S(2)}) async-start(bf16[8,136,512]{2,1,0:T(8,128)(2,1)} %shard_map.179), calls=%async_computation | async-start | bytes 2228224 | tf_op jit(solution)/shard_map/all_to_all | solution.py:705
  18.0 224.9 %all-gather.2.cloned.1.call-start = ((), (), s32[]{:S(2)}) async-start(), calls=%async_computation.5 | async-start | bytes 5640192 | tf_op jit(solution)/shard_map/all_gather | solution.py:697
  24.3 46.2 %collective-permute-start.2 = (bf16[256,1152]{1,0:T(8,128)(2,1)}, bf16[256,1152]{1,0:T(8,128)(2,1)S(1)}, u32[]{:S(2)}, u32[]{:S(2)}) collective-permute-start(bf16[256,1152]{1,0:T(8,128)(2,1)} %shard_map.178.refs_0_), channel_id=1, source_target_pairs={{0,6},{2,0},{4,2},{6,4},{1,7},{3,1},{5,3},{7,5},{8,14},{10,8},{12,... | collective-permute-start | bytes 1769480 | tf_op jit(solution)/shard_map/ppermute | solution.py:618
  28.1 54.2 %collective-permute-start.1 = (bf16[256,1152]{1,0:T(8,128)(2,1)}, bf16[256,1152]{1,0:T(8,128)(2,1)S(1)}, u32[]{:S(2)}, u32[]{:S(2)}) collective-permute-start(bf16[256,1152]{1,0:T(8,128)(2,1)} %shard_map.178.refs_0_), channel_id=1, source_target_pairs={{0,2},{2,4},{4,6},{6,0},{1,3},{3,5},{5,7},{7,1},{8,10},{10,12},{12... | collective-permute-start | bytes 1769480 | tf_op jit(solution)/shard_map/ppermute | solution.py:618
  28.1 54.2 %collective-permute-start = (bf16[256,1152]{1,0:T(8,128)(2,1)}, bf16[256,1152]{1,0:T(8,128)(2,1)}, u32[]{:S(2)}, u32[]{:S(2)}) collective-permute-start(bf16[256,1152]{1,0:T(8,128)(2,1)} %shard_map.178.refs_0_), channel_id=1, source_target_pairs={{0,1},{1,0},{2,3},{3,2},{4,5},{5,4},{6,7},{7,6},{8,9},{9,8},{10,11... | collective-permute-start | bytes 1769480 | tf_op jit(solution)/shard_map/ppermute | solution.py:603
  32.9 392.9 %reduce-scatter.2.cloned.1.call-start = ((), (), s32[]{:S(2)}) async-start(), calls=%async_computation.6 | async-start | bytes 5640192 | tf_op jit(solution)/shard_map/reduce_scatter | solution.py:701
  82.3 57.2 %collective-permute-start.7 = (bf16[1088,512]{1,0:T(8,128)(2,1)S(1)}, bf16[1088,512]{1,0:T(8,128)(2,1)S(1)}, u32[]{:S(2)}, u32[]{:S(2)}) collective-permute-start(bf16[1088,512]{1,0:T(8,128)(2,1)S(1)} %bitcast.53), channel_id=1, source_target_pairs={{0,16},{16,0},{1,17},{17,1},{2,18},{18,2},{3,19},{19,3},{4,20},{20... | collective-permute-start | bytes 3342344 | tf_op jit(solution)/shard_map/ppermute | solution.py:603
  84.3 32.8 %collective-permute-start.5 = (bf16[256,1152]{1,0:T(8,128)(2,1)S(1)}, bf16[256,1152]{1,0:T(8,128)(2,1)S(1)}, u32[]{:S(2)}, u32[]{:S(2)}) collective-permute-start(bf16[256,1152]{1,0:T(8,128)(2,1)S(1)} %collective-permute-done.2.refs_6_), channel_id=1, source_target_pairs={{0,1},{1,0},{2,3},{3,2},{4,5},{5,4},{6,7},{7,6},{8,9},{9,8},{10,11... | collective-permute-start | bytes 1769480 | tf_op jit(solution)/shard_map/ppermute | solution.py:603
  89.0 41.7 %collective-permute-start.6 = (bf16[256,1152]{1,0:T(8,128)(2,1)S(1)}, bf16[256,1152]{1,0:T(8,128)(2,1)}, u32[]{:S(2)}, u32[]{:S(2)}) collective-permute-start(bf16[256,1152]{1,0:T(8,128)(2,1)S(1)} %collective-permute-done.1.refs_2_), channel_id=1, source_target_pairs={{0,2},{2,4},{4,6},{6,0},{1,3},{3,5},{5,7},{7,1},{8,10},{10,12},{12... | collective-permute-start | bytes 1769480 | tf_op jit(solution)/shard_map/ppermute | solution.py:618
  117.0 22.5 %collective-permute-start.4 = (bf16[256,1152]{1,0:T(8,128)(2,1)S(1)}, bf16[256,1152]{1,0:T(8,128)(2,1)S(1)}, u32[]{:S(2)}, u32[]{:S(2)}) collective-permute-start(bf16[256,1152]{1,0:T(8,128)(2,1)S(1)} %collective-permute-done.1.refs_2_), channel_id=1, source_target_pairs={{0,1},{1,0},{2,3},{3,2},{4,5},{5,4},{6,7},{7,6},{8,9},{9,8},{10,11... | collective-permute-start | bytes 1769480 | tf_op jit(solution)/shard_map/ppermute | solution.py:603
  294.6 32.5 %all-to-all-start.2 = ((bf16[8,256,128]{2,1,0:T(8,128)(2,1)}), bf16[8,256,128]{2,1,0:T(8,128)(2,1)}, u32[]{:S(2)}, u32[]{:S(2)}) async-start(bf16[8,256,128]{2,1,0:T(8,128)(2,1)} %get-tuple-element.163), calls=%async_computation.2 | async-start | bytes 1048576 | tf_op jit(solution)/shard_map/all_to_all | solution.py:705
  300.4 26.7 %collective-permute-start.18 = (bf16[1088,384]{1,0:T(8,128)(2,1)S(1)}, bf16[1088,384]{1,0:T(8,128)(2,1)S(1)}, u32[]{:S(2)}, u32[]{:S(2)}) collective-permute-start(bf16[1088,384]{1,0:T(8,128)(2,1)S(1)} %fusion), channel_id=1, source_target_pairs={{0,16},{16,0},{1,17},{17,1},{2,18},{18,2},{3,19},{19,3},{4,20},{20... | collective-permute-start | bytes 2506760 | tf_op jit(solution)/shard_map/ppermute | solution.py:603
  364.0 23.0 %collective-permute-start.21 = (bf16[256,1152]{1,0:T(8,128)(2,1)}, bf16[256,1152]{1,0:T(8,128)(2,1)S(1)}, u32[]{:S(2)}, u32[]{:S(2)}) collective-permute-start(bf16[256,1152]{1,0:T(8,128)(2,1)} %get-tuple-element.175), channel_id=1, source_target_pairs={{0,1},{1,0},{2,3},{3,2},{4,5},{5,4},{6,7},{7,6},{8,9},{9,8},{10,11... | collective-permute-start | bytes 1769480 | tf_op jit(solution)/shard_map/ppermute | solution.py:603
  374.1 39.9 %collective-permute-start.15 = (bf16[2,256,1152]{2,1,0:T(8,128)(2,1)}, bf16[2,256,1152]{2,1,0:T(8,128)(2,1)S(1)}, u32[]{:S(2)}, u32[]{:S(2)}) collective-permute-start(bf16[2,256,1152]{2,1,0:T(8,128)(2,1)} %get-tuple-element.149), channel_id=1, source_target_pairs={{0,8},{8,0},{1,9},{9,1},{2,10},{10,2},{3,11},{11,3},{4,12},{12,4},... | collective-permute-start | bytes 3538952 | tf_op jit(solution)/shard_map/ppermute | solution.py:603
  374.6 25.0 %collective-permute-start.20 = (bf16[256,1152]{1,0:T(8,128)(2,1)S(1)}, bf16[256,1152]{1,0:T(8,128)(2,1)S(1)}, u32[]{:S(2)}, u32[]{:S(2)}) collective-permute-start(bf16[256,1152]{1,0:T(8,128)(2,1)S(1)} %copy-done.33), channel_id=1, source_target_pairs={{0,1},{1,0},{2,3},{3,2},{4,5},{5,4},{6,7},{7,6},{8,9},{9,8},{10,11... | collective-permute-start | bytes 1769480 | tf_op jit(solution)/shard_map/ppermute | solution.py:603
  388.8 33.5 %collective-permute-start.26 = (bf16[256,1152]{1,0:T(8,128)(2,1)}, bf16[256,1152]{1,0:T(8,128)(2,1)}, u32[]{:S(2)}, u32[]{:S(2)}) collective-permute-start(bf16[256,1152]{1,0:T(8,128)(2,1)} %get-tuple-element.183), channel_id=1, source_target_pairs={{0,1},{1,0},{2,3},{3,2},{4,5},{5,4},{6,7},{7,6},{8,9},{9,8},{10,11... | collective-permute-start | bytes 1769480 | tf_op jit(solution)/shard_map/ppermute | solution.py:603
  409.3 47.8 %all-to-all-start.3 = ((bf16[8,136,512]{2,1,0:T(8,128)(2,1)}), bf16[8,136,512]{2,1,0:T(8,128)(2,1)S(1)}, u32[]{:S(2)}, u32[]{:S(2)}) async-start(bf16[8,136,512]{2,1,0:T(8,128)(2,1)} %bitcast.52), calls=%async_computation.3 | async-start | bytes 2228224 | tf_op jit(solution)/shard_map/all_to_all | solution.py:705
  414.9 20.0 %collective-permute-start.29 = (bf16[256,1152]{1,0:T(8,128)(2,1)}, bf16[256,1152]{1,0:T(8,128)(2,1)}, u32[]{:S(2)}, u32[]{:S(2)}) collective-permute-start(bf16[256,1152]{1,0:T(8,128)(2,1)} %fusion.5), channel_id=1, source_target_pairs={{0,16},{16,0},{1,17},{17,1},{2,18},{18,2},{3,19},{19,3},{4,20},{20... | collective-permute-start | bytes 1769480 | tf_op jit(solution)/shard_map/ppermute | solution.py:603
  420.3 18.5 %collective-permute-start.19 = (bf16[256,1152]{1,0:T(8,128)(2,1)}, bf16[256,1152]{1,0:T(8,128)(2,1)}, u32[]{:S(2)}, u32[]{:S(2)}) collective-permute-start(bf16[256,1152]{1,0:T(8,128)(2,1)} %get-tuple-element.171), channel_id=1, source_target_pairs={{0,1},{1,0},{2,3},{3,2},{4,5},{5,4},{6,7},{7,6},{8,9},{9,8},{10,11... | collective-permute-start | bytes 1769480 | tf_op jit(solution)/shard_map/ppermute | solution.py:603
  424.3 23.5 %collective-permute-start.27 = (bf16[256,1152]{1,0:T(8,128)(2,1)}, bf16[256,1152]{1,0:T(8,128)(2,1)}, u32[]{:S(2)}, u32[]{:S(2)}) collective-permute-start(bf16[256,1152]{1,0:T(8,128)(2,1)} %add_convert_fusion), channel_id=1, source_target_pairs={{0,2},{2,4},{4,6},{6,0},{1,3},{3,5},{5,7},{7,1},{8,10},{10,12},{12... | collective-permute-start | bytes 1769480 | tf_op jit(solution)/shard_map/ppermute | solution.py:618
  425.8 31.4 %collective-permute-start.28 = (bf16[136,2304]{1,0:T(8,128)(2,1)}, bf16[136,2304]{1,0:T(8,128)(2,1)S(1)}, u32[]{:S(2)}, u32[]{:S(2)}) collective-permute-start(bf16[136,2304]{1,0:T(8,128)(2,1)} %reduce-scatter.2.cloned.1.call-done.a_ref), channel_id=1, source_target_pairs={{0,16},{16,0},{1,17},{17,1},{2,18},{18,2},{3,19},{19,3},{4,20},{20... | collective-permute-start | bytes 1880072 | tf_op jit(solution)/shard_map/ppermute | solution.py:603
  428.3 28.9 %collective-permute-start.25 = (bf16[256,1152]{1,0:T(8,128)(2,1)}, bf16[256,1152]{1,0:T(8,128)(2,1)}, u32[]{:S(2)}, u32[]{:S(2)}) collective-permute-start(bf16[256,1152]{1,0:T(8,128)(2,1)} %add_convert_fusion.1), channel_id=1, source_target_pairs={{0,6},{2,0},{4,2},{6,4},{1,7},{3,1},{5,3},{7,5},{8,14},{10,8},{12,... | collective-permute-start | bytes 1769480 | tf_op jit(solution)/shard_map/ppermute | solution.py:618
  458.8 32.9 %collective-permute-start.34 = (bf16[2,136,2304]{2,1,0:T(8,128)(2,1)}, bf16[2,136,2304]{2,1,0:T(8,128)(2,1)}, u32[]{:S(2)}, u32[]{:S(2)}) collective-permute-start(bf16[2,136,2304]{2,1,0:T(8,128)(2,1)} %pad_maximum_fusion.1), channel_id=1, source_target_pairs={{0,8},{8,0},{1,9},{9,1},{2,10},{10,2},{3,11},{11,3},{4,12},{12,4},... | collective-permute-start | bytes 3760136 | tf_op jit(solution)/shard_map/ppermute | solution.py:603
  463.0 28.7 %collective-permute-start.33 = (bf16[136,1536]{1,0:T(8,128)(2,1)}, bf16[136,1536]{1,0:T(8,128)(2,1)S(1)}, u32[]{:S(2)}, u32[]{:S(2)}) collective-permute-start(bf16[136,1536]{1,0:T(8,128)(2,1)} %shard_map.189.a_ref), channel_id=1, source_target_pairs={{0,16},{16,0},{1,17},{17,1},{2,18},{18,2},{3,19},{19,3},{4,20},{20... | collective-permute-start | bytes 1253384 | tf_op jit(solution)/shard_map/ppermute | solution.py:603
  (59 other events, 876.3 us)
Sparse Core Ops, SparseCore 0:
  33.0 119.2 all-gather.1
  283.4 117.8 reduce-scatter.1
